TPU v7x, 32 devices: a whole 2x2x4 slice. The times are simulated.
32 devices in a mesh: dp: 8 (over y, x, core), expert: 4 (over z).
Axes of the slice: x: 2, y: 2, z: 4, core: 2. Of those that a mesh axis runs over, the one named last changes fastest.
Arguments:
- tokens: bfloat16 [1024, 4096], P('dp', 'expert'), may hold values from -6 to 6
- output_gradient: bfloat16 [1024, 4096], P('dp', 'expert'), may hold values from -6 to 6
- routing: int32 [1024, 2], P('dp'), may hold values from 0 to 3, all different within a row; in each aligned block of 128 rows (0 to 127, 128 to 255, ...) at most 128 rows name the same one
- router_gate_values: float32 [1024, 2], P('dp'), may hold values from 0.1 to 0.9
- gate_weight: bfloat16 [4, 7168, 4096], P('expert', 'dp'), may hold values from -0.09375 to 0.09375
- up_weight: bfloat16 [4, 7168, 4096], P('expert', 'dp'), may hold values from -0.09375 to 0.09375
- down_weight: bfloat16 [4, 7168, 4096], P('expert', 'dp'), may hold values from -0.0625 to 0.0625
- adapter_lower_gate: bfloat16 [4, 16, 4096], P('expert'), may hold values from -0.09375 to 0.09375
- adapter_upper_gate: bfloat16 [4, 7168, 16], P('expert', 'dp'), may hold values from -0.375 to 0.375
- adapter_lower_up: bfloat16 [4, 16, 4096], P('expert'), may hold values from -0.09375 to 0.09375
- adapter_upper_up: bfloat16 [4, 7168, 16], P('expert', 'dp'), may hold values from -0.375 to 0.375
- adapter_lower_down: bfloat16 [4, 16, 7168], P('expert', None, 'dp'), may hold values from -0.0625 to 0.0625
- adapter_upper_down: bfloat16 [4, 4096, 16], P('expert'), may hold values from -0.375 to 0.375
Outputs:
- grad_x: bfloat16 [1024, 4096], P('dp', 'expert')
- grad_lora_a_gate: float32 [4, 16, 4096], P('expert')
- grad_lora_b_gate: float32 [4, 7168, 16], P('expert', 'dp')
- grad_lora_a_up: float32 [4, 16, 4096], P('expert')
- grad_lora_b_up: float32 [4, 7168, 16], P('expert', 'dp')
- grad_lora_a_down: float32 [4, 16, 7168], P('expert', None, 'dp')
- grad_lora_b_down: float32 [4, 4096, 16], P('expert')
Inputs may be any that keep to these rules, and one draw needn't show every extreme that they name: `routing`: each row names two different experts. In the rows of one dp shard (aligned blocks of 128 rows) no expert is named by more than 128 rows, and in some blocks one expert is named by exactly 128 rows.
All inputs are finite; a program needn't handle non-finite values.
Results may differ from a plain program's by a relative error of at most 0.015.
Values may be sent and summed in bfloat16 or wider, within the bound.
No kernel may reach another device: no remote copies, remote signals or barrier semaphores. Data moves between devices by JAX's collectives and lax.ppermute only.
A program may use at most 256 MiB of HBM per device.

v0:
```python
import jax
import jax.numpy as jnp
from jax import lax
from jax.sharding import PartitionSpec as P

ADAPTER_SCALE = 2.0


def contract_pair(left, right, left_axis, right_axis):
    return lax.dot_general(
        left, right, (((left_axis,), (right_axis,)), ((), ())), preferred_element_type=jnp.float32
    )


def slot_numbers(route_rows, experts):
    picked = (route_rows[:, :, None] == jnp.arange(experts, dtype=jnp.int32)[None, None, :]).astype(
        jnp.int32
    )
    per_token = jnp.sum(picked, axis=1)
    earlier = jnp.cumsum(per_token, axis=0) - per_token
    return jnp.sum(earlier[:, None, :] * picked, axis=2)


def slot_sources(route_rows, positions, experts, capacity):
    tokens_here, choose = route_rows.shape
    target = (route_rows * capacity + positions).reshape(-1)
    owners = jnp.repeat(jnp.arange(tokens_here, dtype=jnp.int32), choose)
    member_ids = jnp.tile(jnp.arange(choose, dtype=jnp.int32), tokens_here)
    source = jnp.full((experts * capacity,), tokens_here, jnp.int32).at[target].set(owners)
    member = jnp.zeros((experts * capacity,), jnp.int32).at[target].set(member_ids)
    return (source, member)


def rows_backward_pass(input_rows, output_gradient_rows, params):
    (
        gate_weight,
        up_weight,
        down_weight,
        a_gate,
        gate_adapter_upper,
        a_up,
        up_adapter_upper,
        down_adapter_lower,
        b_down,
    ) = params
    gate_projected_lower = contract_pair(a_gate, input_rows, 1, 1).astype(jnp.bfloat16)
    up_projected_lower = contract_pair(a_up, input_rows, 1, 1).astype(jnp.bfloat16)
    gate_preactivation = contract_pair(
        gate_weight, input_rows, 1, 1
    ) + ADAPTER_SCALE * contract_pair(gate_adapter_upper, gate_projected_lower, 1, 0)
    up_preactivation = contract_pair(up_weight, input_rows, 1, 1) + ADAPTER_SCALE * contract_pair(
        up_adapter_upper, up_projected_lower, 1, 0
    )
    sigmoid_gate = jax.nn.sigmoid(gate_preactivation)
    silu_gate = gate_preactivation * sigmoid_gate
    hidden_units = (silu_gate * up_preactivation).astype(jnp.bfloat16)
    down_projected_lower = contract_pair(b_down, output_gradient_rows, 0, 1).astype(jnp.bfloat16)
    hidden_gradient = contract_pair(
        down_weight, output_gradient_rows, 1, 1
    ) + ADAPTER_SCALE * contract_pair(down_adapter_lower, down_projected_lower, 0, 0)
    gate_gradient = (
        hidden_gradient
        * up_preactivation
        * sigmoid_gate
        * (1.0 + gate_preactivation * (1.0 - sigmoid_gate))
    ).astype(jnp.bfloat16)
    up_gradient = (hidden_gradient * silu_gate).astype(jnp.bfloat16)
    gate_partial = contract_pair(gate_adapter_upper, gate_gradient, 0, 0).astype(jnp.bfloat16)
    up_partial = contract_pair(up_adapter_upper, up_gradient, 0, 0).astype(jnp.bfloat16)
    down_partial = contract_pair(down_adapter_lower, hidden_units, 1, 0).astype(jnp.bfloat16)
    paired_partials = jnp.concatenate([gate_partial, up_partial], 0)
    paired_factors = jnp.concatenate([a_gate, a_up], 0)
    gradient_rows_out = (
        contract_pair(gate_gradient, gate_weight, 0, 0)
        + contract_pair(up_gradient, up_weight, 0, 0)
        + ADAPTER_SCALE * contract_pair(paired_partials, paired_factors, 0, 0)
    )
    shared_slice = (
        ADAPTER_SCALE * contract_pair(gate_partial, input_rows, 1, 0),
        ADAPTER_SCALE * contract_pair(up_partial, input_rows, 1, 0),
        ADAPTER_SCALE * contract_pair(output_gradient_rows, down_partial, 0, 1),
    )
    owned_slice = (
        ADAPTER_SCALE * contract_pair(gate_gradient, gate_projected_lower, 1, 1),
        ADAPTER_SCALE * contract_pair(up_gradient, up_projected_lower, 1, 1),
        ADAPTER_SCALE * contract_pair(down_projected_lower, hidden_units, 1, 1),
    )
    return (gradient_rows_out, shared_slice, owned_slice)


def local(
    tokens,
    output_gradient,
    routing,
    router_gate_values,
    gate_weight,
    up_weight,
    down_weight,
    adapter_lower_gate,
    adapter_upper_gate,
    adapter_lower_up,
    adapter_upper_up,
    adapter_lower_down,
    adapter_upper_down,
):
    experts = lax.axis_size("expert")
    shards = lax.axis_size("dp")
    tok_local, feat_local = tokens.shape
    choose = routing.shape[1]
    complete_width = feat_local * experts
    capacity = min(tok_local, 6 * tok_local // experts)
    hidden_units_local = gate_weight.shape[1]
    adapter_rank = adapter_lower_gate.shape[1]
    params = (
        gate_weight[0],
        up_weight[0],
        down_weight[0],
        adapter_lower_gate[0],
        adapter_upper_gate[0],
        adapter_lower_up[0],
        adapter_upper_up[0],
        adapter_lower_down[0],
        adapter_upper_down[0],
    )
    positions = slot_numbers(routing, experts)
    zero_row = jnp.zeros((1, feat_local), jnp.bfloat16)
    initial = (
        jnp.zeros((shards * capacity, complete_width), jnp.float32),
        (
            jnp.zeros((adapter_rank, complete_width), jnp.float32),
            jnp.zeros((adapter_rank, complete_width), jnp.float32),
            jnp.zeros((complete_width, adapter_rank), jnp.float32),
        ),
        (
            jnp.zeros((hidden_units_local, adapter_rank), jnp.float32),
            jnp.zeros((hidden_units_local, adapter_rank), jnp.float32),
            jnp.zeros((adapter_rank, hidden_units_local), jnp.float32),
        ),
    )
    source, member = slot_sources(routing, positions, experts, capacity)
    clamped = jnp.minimum(source, tok_local - 1)
    slot_gate = jnp.where(
        source < tok_local, router_gate_values.reshape(-1)[clamped * choose + member], 0.0
    )
    send_x = jnp.concatenate([tokens, zero_row], 0)[source].reshape(experts, capacity, feat_local)
    send_dy = (
        (
            slot_gate[:, None]
            * jnp.concatenate([output_gradient, zero_row], 0)[source].astype(jnp.float32)
        )
        .astype(jnp.bfloat16)
        .reshape(experts, capacity, feat_local)
    )
    recv_x, recv_dy = (
        lax.all_to_all(send_x, "expert", split_axis=0, concat_axis=2, tiled=True),
        lax.all_to_all(send_dy, "expert", split_axis=0, concat_axis=2, tiled=True),
    )
    gradient_rows_out, shared_slice, owned_slice = rows_backward_pass(
        lax.all_gather(recv_x[0], "dp", axis=0, tiled=True),
        lax.all_gather(recv_dy[0], "dp", axis=0, tiled=True),
        params,
    )
    rows_part = gradient_rows_out
    totals = (
        rows_part,
        jax.tree.map(jnp.add, initial[1], shared_slice),
        jax.tree.map(jnp.add, initial[2], owned_slice),
    )
    rows_part, shared_slice, owned_slice = totals
    summed = lax.psum_scatter(
        rows_part.astype(jnp.bfloat16), "dp", scatter_dimension=0, tiled=True
    ).astype(jnp.float32)
    returned_rows = lax.all_to_all(
        summed.reshape(capacity, experts, feat_local).astype(jnp.bfloat16),
        "expert",
        split_axis=1,
        concat_axis=1,
        tiled=True,
    ).astype(jnp.float32)
    lookup = positions * experts + routing
    grad_x = jnp.sum(returned_rows.reshape(capacity * experts, feat_local)[lookup], axis=1).astype(
        jnp.bfloat16
    )
    grad_a_gate, grad_a_up, grad_b_down = (
        lax.psum(shared_slice[0].astype(jnp.bfloat16), "dp").astype(jnp.float32),
        lax.psum(shared_slice[1].astype(jnp.bfloat16), "dp").astype(jnp.float32),
        lax.psum(shared_slice[2].astype(jnp.bfloat16), "dp").astype(jnp.float32),
    )
    return (
        grad_x,
        grad_a_gate[None],
        owned_slice[0][None],
        grad_a_up[None],
        owned_slice[1][None],
        owned_slice[2][None],
        grad_b_down[None],
    )


def solution(mesh):
    return jax.shard_map(
        local,
        mesh=mesh,
        in_specs=(
            P("dp", "expert"),
            P("dp", "expert"),
            P("dp", None),
            P("dp", None),
            P("expert", "dp", None),
            P("expert", "dp", None),
            P("expert", "dp", None),
            P("expert", None, None),
            P("expert", "dp", None),
            P("expert", None, None),
            P("expert", "dp", None),
            P("expert", None, "dp"),
            P("expert", None, None),
        ),
        out_specs=(
            P("dp", "expert"),
            P("expert", None, None),
            P("expert", "dp", None),
            P("expert", None, None),
            P("expert", "dp", None),
            P("expert", None, "dp"),
            P("expert", None, None),
        ),
        check_vma=False,
    )
```

profile of v0, /device:TPU:0, one launch (start us, length us, event | category | flops | bytes accessed | tf_op | source)
XLA Modules:
  0.0 436.5 jit_solution(11069886563797286761)
XLA Ops:
  7.2 0.7 convert_reduce_fusion
  8.3 0.7 select_reduce_fusion
  9.0 1.2 compare_select_fusion.3
  10.5 0.8 copy.39
  11.8 1.4 scatter_custom_fusion.1
  13.2 1.4 scatter_custom_fusion
  14.6 3.5 gather_fusion
  18.1 1.0 concatenate.12
  19.1 2.1 gather_fusion.1
  21.9 31.9 %all_to_all.35 = bf16[4,128,1024]{1,2,0:T(8,128)(2,1)} all-to-all(bf16[4,128,1024]{1,2,0:T(8,128)(2,1)S(1)} %multiply_convert_fusion), channel_id=1, replica_groups=mesh['dp'=8,'expert'=4] {'expert'}, dimensions={0} | all-to-all | bytes 2097152 | tf_op jit(solution)/shard_map/all_to_all | solution.py:156
  54.0 2.1 gather_fusion.2
  56.0 0.7 copy.41
  56.7 28.0 %all_to_all.36 = bf16[4,128,1024]{1,2,0:T(8,128)(2,1)} all-to-all(bf16[4,128,1024]{1,2,0:T(8,128)(2,1)S(1)} %copy.41), channel_id=1, replica_groups=mesh['dp'=8,'expert'=4] {'expert'}, dimensions={0} | all-to-all | bytes 2097152 | tf_op jit(solution)/shard_map/all_to_all | solution.py:155
  84.8 24.3 %all-gather.3.cloned.1.call-done = bf16[1024,4096]{0,1:T(8,128)(2,1)} async-done(((bf16[128,4096]{0,1:T(8,128)(2,1)}), bf16[1024,4096]{0,1:T(8,128)(2,1)}) %all-gather.3.cloned.1.call-update) | async-done | bytes 8388624 | tf_op jit(solution)/shard_map/all_gather | solution.py:160
  109.1 4.6 %convolution_convert_fusion.2 = bf16[1024,16]{0,1:T(8,128)(2,1)S(1)} fusion(bf16[1024,4096]{0,1:T(8,128)(2,1)} %all-gather.3.cloned.1.call-done, bf16[1,4096,16]{1,2,0:T(8,128)(2,1)S(1)} %copy-done), kind=kOutput, calls=%fused_computation.53 | convolution fusion | flops 134234112 | bytes 8552448 | tf_op jit(solution)/shard_map/dot_general | solution.py:10
  113.7 0.6 copy-done.6
  114.3 2.6 fusion.49
  116.9 50.1 %all-gather.5.cloned.1.call-done = bf16[1024,4096]{0,1:T(8,128)(2,1)} async-done(((bf16[128,4096]{0,1:T(8,128)(2,1)}), bf16[1024,4096]{0,1:T(8,128)(2,1)}) %all-gather.5.cloned.1.call-update) | async-done | bytes 8388624 | tf_op jit(solution)/shard_map/all_gather | solution.py:159
  167.0 4.7 %convolution_convert_fusion = bf16[1024,16]{0,1:T(8,128)(2,1)S(1)} fusion(bf16[1024,4096]{0,1:T(8,128)(2,1)} %all-gather.5.cloned.1.call-done, bf16[1,16,4096]{2,1,0:T(8,128)(2,1)S(1)} %copy-done.4), kind=kOutput, calls=%fused_computation.51 | convolution fusion | flops 134234112 | bytes 8552448 | tf_op jit(solution)/shard_map/dot_general | solution.py:10
  171.7 0.6 copy-done.8
  172.3 2.5 fusion.42
  174.9 1.2 convolution_convert_fusion.1
  176.0 2.5 fusion.45
  178.5 13.5 %multiply_add_fusion.2 = f32[1024,896]{1,0:T(8,128)} fusion(f32[1024,896]{1,0:T(8,128)} %fusion.49, bf16[1024,4096]{0,1:T(8,128)(2,1)S(1)} %bitcast.146, bf16[1,896,4096]{2,1,0:T(8,128)(2,1)} %param.19), kind=kOutput, calls=%fused_computation.43 | convolution fusion | flops 7518027776 | bytes 23068672 | tf_op jit(solution)/shard_map/dot_general | solution.py:10
  192.0 13.2 %multiply_add_fusion = f32[1024,896]{1,0:T(8,128)} fusion(f32[1024,896]{1,0:T(8,128)} %fusion.42, bf16[1024,4096]{0,1:T(8,128)(2,1)S(1)} %copy-done.2, bf16[1,896,4096]{2,1,0:T(8,128)(2,1)} %param.17), kind=kOutput, calls=%fused_computation.41 | convolution fusion | flops 7518027776 | bytes 23068672 | tf_op jit(solution)/shard_map/dot_general | solution.py:10
  205.2 18.2 %fusion.23 = (bf16[896,1024]{0,1:T(8,128)(2,1)}, bf16[896,1024]{0,1:T(8,128)(2,1)S(1)}, bf16[896,1024]{0,1:T(8,128)(2,1)S(1)}) fusion(f32[1024,896]{1,0:T(8,128)} %multiply_add_fusion, f32[1024,896]{1,0:T(8,128)} %multiply_add_fusion.2, f32[1024,896]{1,0:T(8,128)} %fusion.45, bf16[1024,4096]{0,1:T(8,128)(2,1)} %all-gather.5.cloned.1.call-done, ...), kind=kOutput, calls=%fused_computation.38 | convolution fusion | flops 7531790336 | bytes 32243712 | tf_op jit(solution)/shard_map/dot_general | solution.py:10
  224.0 14.4 %fusion.4 = f32[1024,4096]{1,0:T(8,128)} fusion(bf16[896,1024]{0,1:T(8,128)(2,1)S(1)} %get-tuple-element.12, bf16[1,896,4096]{2,1,0:T(8,128)(2,1)} %param.18), kind=kOutput, calls=%fused_computation.11 | convolution fusion | flops 7516192768 | bytes 25952256 | tf_op jit(solution)/shard_map/dot_general | solution.py:10
  239.0 14.4 %fusion = f32[1024,4096]{1,0:T(8,128)} fusion(bf16[896,1024]{0,1:T(8,128)(2,1)S(1)} %get-tuple-element.11, bf16[1,896,4096]{2,1,0:T(8,128)(2,1)} %param.17), kind=kOutput, calls=%fused_computation.7 | convolution fusion | flops 7516192768 | bytes 25952256 | tf_op jit(solution)/shard_map/dot_general | solution.py:10
  253.4 15.7 %add_convert_fusion = bf16[1024,4096]{1,0:T(8,128)(2,1)} fusion(f32[1024,4096]{1,0:T(8,128)} %fusion, f32[1024,4096]{1,0:T(8,128)} %fusion.4, bf16[16,4096]{1,0:T(8,128)(2,1)S(1)} %bitcast.153, bf16[16,4096]{1,0:T(8,128)(2,1)S(1)} %bitcast.152, bf16[16,1024]{1,0:T(8,128)(2,1)S(1)} %bitcast.156, bf16[16,1024]{1,0:T(8,128)(2,1)S(1)} %bitcast.155), kind=kOutput, calls=%fused_computation.6 | convolution fusion | flops 285868032 | bytes 42270720 | tf_op jit(solution)/shard_map/dot_general | solution.py:10
  269.1 0.7 copy-done.15
  270.0 6.3 %fusion.14 = bf16[1,16,4096]{2,1,0:T(8,128)(2,1)} fusion(bf16[1024,16]{0,1:T(8,128)(2,1)S(1)} %convolution_convert_fusion.4, bf16[1024,4096]{0,1:T(8,128)(2,1)} %all-gather.5.cloned.1.call-done), kind=kOutput, calls=%fused_computation.24 | convolution fusion | flops 134348800 | bytes 8552448 | tf_op jit(solution)/shard_map/dot_general | solution.py:10
  276.4 64.2 %reduce-scatter.2.cloned.1.call-done = bf16[128,4096]{1,0:T(8,128)(2,1)} async-done(((bf16[1024,4096]{1,0:T(8,128)(2,1)}), bf16[128,4096]{1,0:T(8,128)(2,1)}) %reduce-scatter.2.cloned.1.call-update) | async-done | bytes 1048592 | tf_op jit(solution)/shard_map/reduce_scatter | solution.py:170
  340.5 2.3 copy.47
  342.8 4.6 %all-to-all-start.2 = ((bf16[128,4,1024]{2,0,1:T(8,128)(2,1)}), bf16[128,4,1024]{2,0,1:T(8,128)(2,1)S(1)}, u32[]{:S(2)}, u32[]{:S(2)}) async-start(bf16[128,4,1024]{2,0,1:T(8,128)(2,1)} %bitcast.149), calls=%async_computation.3 | async-start | bytes 2097152 | tf_op jit(solution)/shard_map/all_to_all | solution.py:173
  347.4 6.3 %fusion.15 = bf16[1,16,4096]{2,1,0:T(8,128)(2,1)} fusion(bf16[1024,16]{0,1:T(8,128)(2,1)S(1)} %convolution_convert_fusion.5, bf16[1024,4096]{0,1:T(8,128)(2,1)} %all-gather.5.cloned.1.call-done), kind=kOutput, calls=%fused_computation.25 | convolution fusion | flops 134348800 | bytes 8552448 | tf_op jit(solution)/shard_map/dot_general | solution.py:10
  353.8 7.3 %fusion.13 = bf16[1,4096,16]{1,2,0:T(8,128)(2,1)} fusion(bf16[1024,4096]{0,1:T(8,128)(2,1)} %all-gather.3.cloned.1.call-done, bf16[896,1024]{0,1:T(8,128)(2,1)} %get-tuple-element.10, bf16[1,16,896]{2,1,0:T(8,128)(2,1)S(1)} %copy-done.14), kind=kOutput, calls=%fused_computation.23 | convolution fusion | flops 163725312 | bytes 10383360 | tf_op jit(solution)/shard_map/dot_general | solution.py:10
  361.1 2.5 fusion.33
  363.6 2.5 fusion.32
  366.1 1.0 fusion.31
  367.0 49.3 %all-reduce.5.cloned.1.call-done = (bf16[1,16,4096]{2,1,0:T(8,128)(2,1)}, bf16[1,16,4096]{2,1,0:T(8,128)(2,1)}, bf16[1,4096,16]{1,2,0:T(8,128)(2,1)}) async-done(((bf16[1,16,4096]{2,1,0:T(8,128)(2,1)}, bf16[1,16,4096]{2,1,0:T(8,128)(2,1)}, bf16[1,4096,16]{1,2,0:T(8,128)(2,1)}), (bf16[1,16,4096]{2,1,0:T(8,128)(2,1)}, bf16[1,16,4096]{2,1,0:T(8,128)(2,1)}, ...) | async-done | bytes 393232 | tf_op jit(solution)/shard_map/psum | solution.py:185
  416.4 1.6 broadcast_in_dim.57
  418.0 1.6 broadcast_in_dim.60
  419.6 1.6 broadcast_in_dim.64
  421.2 2.1 copy.43
  423.4 2.2 reshape.92
  425.7 1.1 gather_fusion.3
  426.7 0.6 reshape.122
  427.4 2.1 reduce_sum.29
  (66 shorter events, 3.4 us)
Async XLA Ops:
  7.2 101.9 %copy-start = (bf16[1,4096,16]{1,2,0:T(8,128)(2,1)S(1)}, bf16[1,4096,16]{1,2,0:T(8,128)(2,1)}, u32[]{:S(2)}) copy-start(bf16[1,4096,16]{1,2,0:T(8,128)(2,1)} %param.25) | copy-start | bytes 393220
  7.2 101.9 %all-gather.3.cloned.1.call-start = ((), (), s32[]{:S(2)}) async-start(), calls=%async_computation.4 | async-start | bytes 9437184 | tf_op jit(solution)/shard_map/all_gather | solution.py:160
  21.7 32.2 %copy-start.10 = (bf16[128,1024]{1,0:T(8,128)(2,1)S(1)}, bf16[128,1024]{1,0:T(8,128)(2,1)}, u32[]{:S(2)}) copy-start(bf16[128,1024]{1,0:T(8,128)(2,1)} %param.13) | copy-start | bytes 786436
  53.9 113.1 %all-gather.5.cloned.1.call-start = ((), (), s32[]{:S(2)}) async-start(), calls=%async_computation.5 | async-start | bytes 9437184 | tf_op jit(solution)/shard_map/all_gather | solution.py:159
  84.7 29.6 %copy-start.13 = (bf16[1,16,896]{2,1,0:T(8,128)(2,1)S(1)}, bf16[1,16,896]{2,1,0:T(8,128)(2,1)}, u32[]{:S(2)}) copy-start(bf16[1,16,896]{2,1,0:T(8,128)(2,1)} %param.24) | copy-start | bytes 86020
  84.8 255.8 %reduce-scatter.2.cloned.1.call-start = ((), (), s32[]{:S(2)}) async-start(), calls=%async_computation.6 | async-start | bytes 9437184 | tf_op jit(solution)/shard_map/reduce_scatter | solution.py:170
  113.7 0.6 copy-start.6
  114.3 52.7 %copy-start.4 = (bf16[1,16,4096]{2,1,0:T(8,128)(2,1)S(1)}, bf16[1,16,4096]{2,1,0:T(8,128)(2,1)}, u32[]{:S(2)}) copy-start(bf16[1,16,4096]{2,1,0:T(8,128)(2,1)} %param.20) | copy-start | bytes 393220
  116.9 55.4 %copy-start.12 = (bf16[1,896,16]{1,2,0:T(8,128)(2,1)S(1)}, bf16[1,896,16]{1,2,0:T(8,128)(2,1)}, u32[]{:S(2)}) copy-start(bf16[1,896,16]{1,2,0:T(8,128)(2,1)} %param.21) | copy-start | bytes 86020
  167.0 7.9 %copy-start.2 = (bf16[1024,4096]{0,1:T(8,128)(2,1)S(1)}, bf16[1024,4096]{0,1:T(8,128)(2,1)}, u32[]{:S(2)}) copy-start(bf16[1024,4096]{0,1:T(8,128)(2,1)} %all-gather.5.cloned.1.call-done) | copy-start | bytes 25165828
  167.0 7.9 %copy-start.5 = (bf16[1,16,4096]{2,1,0:T(8,128)(2,1)S(1)}, bf16[1,16,4096]{2,1,0:T(8,128)(2,1)}, u32[]{:S(2)}) copy-start(bf16[1,16,4096]{2,1,0:T(8,128)(2,1)} %param.22) | copy-start | bytes 393220
  171.7 0.6 copy-start.8
  172.3 6.2 %slice-start = ((s8[8388608]{0:T(1024)(128)(4,1)}), s8[4194304]{0:T(1024)(128)(4,1)S(1)}, s32[]{:S(2)}) async-start(s8[8388608]{0:T(1024)(128)(4,1)} %bitcast.145), calls=%async_computation.8 | async-start | bytes 8388608
  174.8 1.2 copy-start.11
  174.8 3.7 slice-start.1
  223.5 15.5 %copy-start.3 = (bf16[896,1024]{0,1:T(8,128)(2,1)}, bf16[896,1024]{0,1:T(8,128)(2,1)S(1)}, u32[]{:S(2)}) copy-start(bf16[896,1024]{0,1:T(8,128)(2,1)S(1)} %get-tuple-element.11) | copy-start | bytes 5505028
  269.1 0.7 copy-start.15
  342.8 78.4 %all-to-all-start.2 = ((bf16[128,4,1024]{2,0,1:T(8,128)(2,1)}), bf16[128,4,1024]{2,0,1:T(8,128)(2,1)S(1)}, u32[]{:S(2)}, u32[]{:S(2)}) async-start(bf16[128,4,1024]{2,0,1:T(8,128)(2,1)} %bitcast.149), calls=%async_computation.3 | async-start | bytes 2097152 | tf_op jit(solution)/shard_map/all_to_all | solution.py:173
  347.4 6.3 %copy-start.14 = (bf16[1,16,896]{2,1,0:T(8,128)(2,1)S(1)}, bf16[1,16,896]{2,1,0:T(8,128)(2,1)}, u32[]{:S(2)}) copy-start(bf16[1,16,896]{2,1,0:T(8,128)(2,1)} %param.24) | copy-start | bytes 86020
  347.4 68.9 %all-reduce.5.cloned.1.call-start = ((), (), s32[]{:S(2)}) async-start(), calls=%async_computation.7 | async-start | bytes 786432 | tf_op jit(solution)/shard_map/psum | solution.py:185
  353.8 7.3 %copy-start.7 = (bf16[1024,16]{0,1:T(8,128)(2,1)S(1)}, bf16[1024,16]{0,1:T(8,128)(2,1)}, u32[]{:S(2)}) copy-start(bf16[1024,16]{0,1:T(8,128)(2,1)} %copy-done.6) | copy-start | bytes 98308
  353.8 9.8 %copy-start.9 = (bf16[1024,16]{0,1:T(8,128)(2,1)S(1)}, bf16[1024,16]{0,1:T(8,128)(2,1)}, u32[]{:S(2)}) copy-start(bf16[1024,16]{0,1:T(8,128)(2,1)} %copy-done.8) | copy-start | bytes 98308
  425.6 3.8 copy-start.1
Sparse Core Ops, SparseCore 0:
  54.0 55.0 all-gather.2
  111.0 55.9 all-gather.4
  269.2 71.2 reduce-scatter.1
  361.2 55.1 all-reduce.4
where the time goes:
time: 445 us; the launch traced here: 436 us
  waiting for transfers between devices  188 us (42%)
  matrix products  135 us (30%)
  blocking collectives  60 us (13%)
  local copies, waits for them, and re-layouts  24.8 us (6%)
  between operations  14.5 us (3%)
  other arithmetic  10 us (2%)
  starting transfers between devices  4.72 us (1%)
    dot_general x20, matrix products, contract_pair(): lax.dot_general(left, right, (((left_axis,), (right_axis,)), ((), ())), p...  135 us
    reduce_scatter x1, waiting for transfers between devices, local(): lax.psum_scatter(rows_part.astype(jnp.bfloat16), 'dp', scatter_dimension=...  64.2 us
    all_gather x1, waiting for transfers between devices, local(): lax.all_gather(recv_x[0], 'dp', axis=0, tiled=True)  50.1 us
    psum x1, waiting for transfers between devices, local(): lax.psum(shared_slice[0].astype(jnp.bfloat16), 'dp').astype(jnp.float32)  49.3 us
    all_to_all x1, blocking collectives, local(): lax.all_to_all(send_dy, 'expert', split_axis=0, concat_axis=2, tiled=True)  31.9 us
    all_to_all x1, blocking collectives, local(): lax.all_to_all(send_x, 'expert', split_axis=0, concat_axis=2, tiled=True)  28 us
    all_gather x1, waiting for transfers between devices, local(): lax.all_gather(recv_dy[0], 'dp', axis=0, tiled=True)  24.3 us
  transfers between devices with their start and end apart: 5, of which 4 were waited for; matrix products, arithmetic and copies ran while one was open for 9% of the time, Pallas kernels for 0%

commit v1 on v0

--- a/solution.py
+++ b/solution.py
@@ -1,6 +1,8 @@
 import jax
 import jax.numpy as jnp
 from jax import lax
+from jax.experimental import pallas as pl
+from jax.experimental.pallas import tpu as pltpu
 from jax.sharding import PartitionSpec as P
 
 ADAPTER_SCALE = 2.0
@@ -88,7 +90,7 @@
     return (gradient_rows_out, shared_slice, owned_slice)
 
 
-def local(
+def general_local(
     tokens,
     output_gradient,
     routing,
@@ -197,9 +199,537 @@
     )
 
 
+LANES = 128
+TILE = 256
+SHARDS = 8
+VMEM_BYTES = 58 * 1024 * 1024
+HBM = pl.BlockSpec(memory_space=pl.ANY)
+VMEM = pl.BlockSpec(memory_space=pltpu.VMEM)
+SMEM = pl.BlockSpec(memory_space=pltpu.SMEM)
+
+
+def dot_nt(left, right):
+    return contract_pair(left, right, 1, 1)
+
+
+def dot_nn(left, right):
+    return contract_pair(left, right, 1, 0)
+
+
+def forward_kernel(
+    n_pieces,
+    *refs,
+):
+    pieces = refs[:n_pieces]
+    (gate_hbm, up_hbm, lower_ref, upper_ref, silu_out, slope_out, hidden_out, low_out) = refs[
+        n_pieces : n_pieces + 8
+    ]
+    x_rows, weights, x_sems, w_sems = refs[n_pieces + 8 :]
+    per_block = n_pieces // SHARDS
+    deep, tokens_each, feat = pieces[0].shape
+    tiles = weights.shape[0]
+    rows = x_rows.shape[0]
+    x_copies = []
+    for i, piece in enumerate(pieces):
+        block, part = divmod(i, per_block)
+        for z in range(deep):
+            at = part * deep + z
+            x_copies.append(
+                pltpu.make_async_copy(
+                    piece.at[z],
+                    x_rows.at[pl.ds(block * tokens_each, tokens_each), pl.ds(at * feat, feat)],
+                    x_sems.at[i * deep + z],
+                )
+            )
+
+    def weight_copies(tile):
+        source = pl.ds(pl.multiple_of(tile * LANES, LANES), LANES)
+        return (
+            pltpu.make_async_copy(
+                gate_hbm.at[source], weights.at[tile, pl.ds(0, LANES)], w_sems.at[tile, 0]
+            ),
+            pltpu.make_async_copy(
+                up_hbm.at[source], weights.at[tile, pl.ds(LANES, LANES)], w_sems.at[tile, 1]
+            ),
+        )
+
+    for copy in x_copies:
+        copy.start()
+    for tile in range(tiles):
+        for copy in weight_copies(tile):
+            copy.start()
+    for copy in x_copies:
+        copy.wait()
+    half = rows // 2
+    for m in range(2):
+        at = pl.ds(m * half, half)
+        low_out[at, :] = dot_nt(x_rows[at, :], lower_ref[...]).astype(jnp.bfloat16)
+
+    @pl.loop(0, tiles)
+    def _(tile):
+        for copy in weight_copies(tile):
+            copy.wait()
+        lanes = pl.ds(pl.multiple_of(tile * LANES, LANES), LANES)
+
+        @pl.loop(0, 2)
+        def _(m):
+            at = pl.ds(pl.multiple_of(m * half, half), half)
+            pre = dot_nt(x_rows[at, :], weights[tile])
+            pre = pre + ADAPTER_SCALE * dot_nn(low_out[at, :], upper_ref[tile])
+            pre_gate, pre_up = pre[:, :LANES], pre[:, LANES:]
+            sigma = 1.0 / (1.0 + jnp.exp(-pre_gate))
+            silu = pre_gate * sigma
+            silu_out[at, lanes] = silu
+            slope_out[at, lanes] = pre_up * (sigma * (1.0 + pre_gate * (1.0 - sigma)))
+            hidden_out[at, lanes] = (silu * pre_up).astype(jnp.bfloat16)
+
+
+def forward_rows(pieces, gate_weight, up_weight, lower_cat, upper_tiles):
+    hidden_here, width = gate_weight.shape
+    rows = SHARDS * pieces[0].shape[1]
+    rank2 = lower_cat.shape[0]
+    tiles = hidden_here // LANES
+    copies = len(pieces) * pieces[0].shape[0]
+    flops = 4 * rows * hidden_here * width
+    return pl.pallas_call(
+        lambda *refs: forward_kernel(len(pieces), *refs),
+        out_shape=(
+            jax.ShapeDtypeStruct((rows, hidden_here), jnp.float32),
+            jax.ShapeDtypeStruct((rows, hidden_here), jnp.float32),
+            jax.ShapeDtypeStruct((rows, hidden_here), jnp.bfloat16),
+            jax.ShapeDtypeStruct((rows, rank2), jnp.bfloat16),
+        ),
+        in_specs=[HBM] * (len(pieces) + 2) + [VMEM] * 2,
+        out_specs=(VMEM,) * 4,
+        scratch_shapes=[
+            pltpu.VMEM((rows, width), jnp.bfloat16),
+            pltpu.VMEM((tiles, 2 * LANES, width), jnp.bfloat16),
+            pltpu.SemaphoreType.DMA((copies,)),
+            pltpu.SemaphoreType.DMA((tiles, 2)),
+        ],
+        compiler_params=pltpu.CompilerParams(vmem_limit_bytes=VMEM_BYTES),
+        cost_estimate=pl.CostEstimate(
+            flops=flops, bytes_accessed=40_000_000, transcendentals=rows * hidden_here
+        ),
+        name="forward_rows",
+    )(*pieces, gate_weight, up_weight, lower_cat, upper_tiles)
+
+
+def backward_kernel(
+    n_pieces,
+    row_start,
+    *refs,
+):
+    pieces = refs[:n_pieces]
+    (
+        route_ref,
+        gate_hbm,
+        up_hbm,
+        down_hbm,
+        down_upper_ref,
+        down_lower_ref,
+        gate_upper_ref,
+        up_upper_ref,
+        silu_hbm,
+        slope_hbm,
+        hidden_hbm,
+        low_hbm,
+        keep_out,
+        pass_out,
+        parts_out,
+        owned_out,
+    ) = refs[n_pieces : n_pieces + 16]
+    (g_rows, down_w, pair_w, d_pair, silu, slope, hidden, low, in_sems, d_sems, p_sems, f_sems) = refs[
+        n_pieces + 16 :
+    ]
+    deep, tokens_each, feat = pieces[0].shape
+    rows, width = g_rows.shape
+    hidden_here = silu.shape[1]
+    rank = down_upper_ref.shape[0]
+    per_block = n_pieces // 2
+    copies = []
+    for i, piece in enumerate(pieces):
+        block, part = divmod(i, per_block)
+        for z in range(deep):
+            at = part * deep + z
+            copies.append(
+                pltpu.make_async_copy(
+                    piece.at[z],
+                    g_rows.at[pl.ds(block * tokens_each, tokens_each), pl.ds(at * feat, feat)],
+                    in_sems.at[i * deep + z],
+                )
+            )
+    tiles = [(at, min(TILE, hidden_here - at)) for at in range(0, hidden_here, TILE)]
+    down_copies = [
+        pltpu.make_async_copy(down_hbm.at[pl.ds(at, n)], down_w.at[pl.ds(at, n)], d_sems.at[i])
+        for i, (at, n) in enumerate(tiles)
+    ]
+    up_factor_copy = pltpu.make_async_copy(
+        down_upper_ref, down_w.at[pl.ds(hidden_here, rank)], d_sems.at[len(tiles)]
+    )
+    here = pl.ds(row_start, rows)
+    saved_copies = [
+        pltpu.make_async_copy(source.at[here], target, f_sems.at[i])
+        for i, (source, target) in enumerate(
+            ((silu_hbm, silu), (slope_hbm, slope), (hidden_hbm, hidden), (low_hbm, low))
+        )
+    ]
+    slabs = width // feat
+
+    def pair_copies(slab):
+        columns = pl.ds(slab * feat, feat)
+        return (
+            pltpu.make_async_copy(
+                gate_hbm.at[:, columns], pair_w.at[slab, pl.ds(0, hidden_here)], p_sems.at[slab, 0]
+            ),
+            pltpu.make_async_copy(
+                up_hbm.at[:, columns],
+                pair_w.at[slab, pl.ds(hidden_here, hidden_here)],
+                p_sems.at[slab, 1],
+            ),
+        )
+
+    for copy in copies + [up_factor_copy] + down_copies[::-1] + saved_copies:
+        copy.start()
+    for slab in range(slabs):
+        for copy in pair_copies(slab):
+            copy.start()
+    for copy in copies:
+        copy.wait()
+
+    @pl.loop(0, width // feat)
+    def _(z):
+        lanes = pl.ds(pl.multiple_of(z * feat, feat), feat)
+        g_rows[:, lanes] = (route_ref[...] * g_rows[:, lanes].astype(jnp.float32)).astype(
+            jnp.bfloat16
+        )
+
+    up_factor_copy.wait()
+    low_down = None
+    for i in reversed(range(len(tiles))):
+        at, n = tiles[i]
+        down_copies[i].wait()
+        last = i == len(tiles) - 1
+        whole = dot_nt(g_rows[...], down_w[at : at + n + (rank if last else 0), :])
+        if last:
+            low_down = whole[:, n:].astype(jnp.bfloat16)
+            for copy in saved_copies:
+                copy.wait()
+        d_hidden = whole[:, :n] + ADAPTER_SCALE * dot_nn(low_down, down_lower_ref[:, at : at + n])
+        d_pair[:, at : at + n] = (d_hidden * slope[:, at : at + n]).astype(jnp.bfloat16)
+        d_pair[:, hidden_here + at : hidden_here + at + n] = (
+            d_hidden * silu[:, at : at + n]
+        ).astype(jnp.bfloat16)
+    for slab in range(slabs):
+        for copy in pair_copies(slab):
+            copy.wait()
+
+        @pl.loop(0, feat // TILE)
+        def _(n):
+            lanes = pl.ds(pl.multiple_of(n * TILE, TILE), TILE)
+            term = dot_nn(d_pair[...], pair_w[slab, :, lanes]).astype(jnp.bfloat16)
+            keep_out[slab, :, lanes] = term[:tokens_each]
+            pass_out[slab, :, lanes] = term[tokens_each:]
+
+    d_gate, d_up = d_pair[:, :hidden_here], d_pair[:, hidden_here:]
+    parts_out[0:rank, :] = dot_nt(gate_upper_ref[...], d_gate)
+    parts_out[rank : 2 * rank, :] = dot_nt(up_upper_ref[...], d_up)
+    parts_out[2 * rank :, :] = dot_nt(down_lower_ref[...], hidden[...])
+    owned_out[0] = ADAPTER_SCALE * contract_pair(low[:, :rank], d_gate, 0, 0)
+    owned_out[1] = ADAPTER_SCALE * contract_pair(low[:, rank:], d_up, 0, 0)
+    owned_out[2] = ADAPTER_SCALE * contract_pair(low_down, hidden[...], 0, 0)
+
+
+def backward_rows(
+    pieces,
+    row_start,
+    route_rows,
+    weights,
+    down_upper,
+    down_lower,
+    gate_upper,
+    up_upper,
+    saved,
+):
+    hidden_here, width = weights[0].shape
+    rank = down_upper.shape[0]
+    deep, tokens_each, feat = pieces[0].shape
+    rows = 2 * tokens_each
+    slabs = width // feat
+    term = jax.ShapeDtypeStruct((slabs, tokens_each, feat), jnp.bfloat16)
+    return pl.pallas_call(
+        lambda *refs: backward_kernel(len(pieces), row_start, *refs),
+        out_shape=(
+            term,
+            term,
+            jax.ShapeDtypeStruct((3 * rank, rows), jnp.float32),
+            jax.ShapeDtypeStruct((3, rank, hidden_here), jnp.float32),
+        ),
+        in_specs=[HBM] * len(pieces)
+        + [VMEM]
+        + [HBM] * 3
+        + [VMEM] * 4
+        + [HBM] * 4,
+        out_specs=(VMEM,) * 4,
+        scratch_shapes=[
+            pltpu.VMEM((rows, width), jnp.bfloat16),
+            pltpu.VMEM((hidden_here + rank, width), jnp.bfloat16),
+            pltpu.VMEM((slabs, 2 * hidden_here, feat), jnp.bfloat16),
+            pltpu.VMEM((rows, 2 * hidden_here), jnp.bfloat16),
+            pltpu.VMEM((rows, hidden_here), jnp.float32),
+            pltpu.VMEM((rows, hidden_here), jnp.float32),
+            pltpu.VMEM((rows, hidden_here), jnp.bfloat16),
+            pltpu.VMEM((rows, 2 * rank), jnp.bfloat16),
+            pltpu.SemaphoreType.DMA((len(pieces) * deep,)),
+            pltpu.SemaphoreType.DMA((pl.cdiv(hidden_here, TILE) + 1,)),
+            pltpu.SemaphoreType.DMA((slabs, 2)),
+            pltpu.SemaphoreType.DMA((4,)),
+        ],
+        compiler_params=pltpu.CompilerParams(vmem_limit_bytes=VMEM_BYTES),
+        cost_estimate=pl.CostEstimate(
+            flops=6 * rows * hidden_here * width,
+            bytes_accessed=6 * hidden_here * width + 4 * rows * width,
+            transcendentals=0,
+        ),
+        name="backward_rows",
+    )(*pieces, route_rows, *weights, down_upper, down_lower, gate_upper, up_upper, *saved)
+
+
+def shared_kernel(n_pieces, *refs):
+    x_pieces, dy_pieces = refs[:n_pieces], refs[n_pieces : 2 * n_pieces]
+    order_ref, sums_ref, down_sums_ref, pair_out, down_out = refs[2 * n_pieces : 2 * n_pieces + 5]
+    x_rows, dy_rows, sums, down_sums, sems = refs[2 * n_pieces + 5 :]
+    deep, tokens_each, feat = x_pieces[0].shape
+    per_block = n_pieces // SHARDS
+    copies = []
+    for side, (pieces, target) in enumerate(((x_pieces, x_rows), (dy_pieces, dy_rows))):
+        for i, piece in enumerate(pieces):
+            block, part = divmod(i, per_block)
+            start = pl.multiple_of(order_ref[block] * tokens_each, tokens_each)
+            for z in range(deep):
+                at = part * deep + z
+                copies.append(
+                    pltpu.make_async_copy(
+                        piece.at[z],
+                        target.at[pl.ds(start, tokens_each), pl.ds(at * feat, feat)],
+                        sems.at[side, i * deep + z],
+                    )
+                )
+    for copy in copies:
+        copy.start()
+    for block in range(SHARDS):
+        lanes = pl.ds(pl.multiple_of(order_ref[block] * tokens_each, tokens_each), tokens_each)
+        sums[:, lanes] = sums_ref[block]
+        down_sums[:, lanes] = down_sums_ref[block]
+    for copy in copies:
+        copy.wait()
+    width = x_rows.shape[1]
+    step = 2 * TILE
+
+    @pl.loop(0, width // step)
+    def _(n):
+        lanes = pl.ds(pl.multiple_of(n * step, step), step)
+        pair_out[:, lanes] = ADAPTER_SCALE * dot_nn(
+            sums[...].astype(jnp.bfloat16), x_rows[:, lanes]
+        )
+        down_out[:, lanes] = ADAPTER_SCALE * dot_nn(
+            down_sums[...].astype(jnp.bfloat16), dy_rows[:, lanes]
+        )
+
+
+def shared_gradients(x_pieces, dy_pieces, order, sums, down_sums):
+    deep, tokens_each, feat = x_pieces[0].shape
+    n_pieces = len(x_pieces)
+    width = deep * feat * n_pieces // SHARDS
+    rows = SHARDS * tokens_each
+    pair, rank = sums.shape[1], down_sums.shape[1]
+    return pl.pallas_call(
+        lambda *refs: shared_kernel(n_pieces, *refs),
+        out_shape=(
+            jax.ShapeDtypeStruct((pair, width), jnp.float32),
+            jax.ShapeDtypeStruct((rank, width), jnp.float32),
+        ),
+        in_specs=[HBM] * (2 * n_pieces) + [SMEM, VMEM, VMEM],
+        out_specs=(VMEM, VMEM),
+        scratch_shapes=[
+            pltpu.VMEM((rows, width), jnp.bfloat16),
+            pltpu.VMEM((rows, width), jnp.bfloat16),
+            pltpu.VMEM((pair, rows), jnp.float32),
+            pltpu.VMEM((rank, rows), jnp.float32),
+            pltpu.SemaphoreType.DMA((2, n_pieces * deep)),
+        ],
+        compiler_params=pltpu.CompilerParams(vmem_limit_bytes=VMEM_BYTES),
+        cost_estimate=pl.CostEstimate(
+            flops=16 * rows * pair * width, bytes_accessed=4 * rows * width, transcendentals=0
+        ),
+        name="shared_gradients",
+    )(*x_pieces, *dy_pieces, order, sums, down_sums)
+
+
+CORE, ACROSS, ALONG = 1, 2, 4
+
+
+def swap(value, bit):
+    return lax.ppermute(value, "dp", [(i, i ^ bit) for i in range(SHARDS)])
+
+
+def spread(block):
+    half = block.shape[0] // 2
+    lo, hi = block[:half], block[half:]
+    along_lo, across_hi = swap(lo, ALONG), swap(hi, ACROSS)
+    across_lo, along_hi = swap(lo, ACROSS), swap(hi, ALONG)
+    far_lo, far_hi = swap(along_lo, ACROSS), swap(across_hi, ALONG)
+    near = [(lo, hi), (across_lo, across_hi), (along_lo, along_hi), (far_lo, far_hi)]
+    blocks = []
+    for pair in near:
+        blocks.append(pair)
+        blocks.append(tuple(swap(part, CORE) for part in pair))
+    return blocks
+
+
+def added(left, right):
+    return (left.astype(jnp.float32) + right.astype(jnp.float32)).astype(jnp.bfloat16)
+
+
+def local(
+    tokens,
+    output_gradient,
+    routing,
+    router_gate_values,
+    gate_weight,
+    up_weight,
+    down_weight,
+    adapter_lower_gate,
+    adapter_upper_gate,
+    adapter_lower_up,
+    adapter_upper_up,
+    adapter_lower_down,
+    adapter_upper_down,
+):
+    experts = lax.axis_size("expert")
+    me, expert = lax.axis_index("dp"), lax.axis_index("expert")
+    tokens_each, feat = tokens.shape
+    hidden_here = gate_weight.shape[1]
+    rank = adapter_lower_gate.shape[1]
+    tiles = hidden_here // LANES
+    order = jnp.bitwise_xor(jnp.arange(SHARDS, dtype=jnp.int32), me.astype(jnp.int32))
+
+    named = routing[:, :, None] == jnp.arange(experts, dtype=jnp.int32)[None, None, :]
+    weight_of = jnp.sum(jnp.where(named, router_gate_values[:, :, None], 0.0), axis=1)
+    all_routes = lax.all_gather(weight_of.T, "dp", axis=0, tiled=False)
+    route = lax.dynamic_index_in_dim(all_routes, expert, axis=1, keepdims=False)[order]
+    route_column = route.reshape(SHARDS * tokens_each, 1)
+
+    lower_cat = jnp.concatenate([adapter_lower_gate[0], adapter_lower_up[0]], axis=0)
+    gate_upper, up_upper = adapter_upper_gate[0].T, adapter_upper_up[0].T
+    nothing = jnp.zeros((rank, tiles, LANES), jnp.bfloat16)
+    upper_tiles = jnp.concatenate(
+        [
+            jnp.concatenate([gate_upper.reshape(rank, tiles, LANES), nothing], axis=2),
+            jnp.concatenate([nothing, up_upper.reshape(rank, tiles, LANES)], axis=2),
+        ],
+        axis=0,
+    ).transpose(1, 0, 2)
+    down_upper = adapter_upper_down[0].T
+    down_lower = adapter_lower_down[0]
+
+    x_here = lax.all_gather(tokens, "expert", axis=0, tiled=False)
+    dy_here = lax.all_gather(output_gradient, "expert", axis=0, tiled=False)
+    x_blocks = spread(x_here)
+    x_tail = [x_blocks[2], x_blocks[4]]
+    dy_here, x_tail = lax.optimization_barrier((dy_here, x_tail))
+    x_blocks[2], x_blocks[4] = x_tail
+    dy_blocks = spread(dy_here)
+    x_pieces = [part for pair in x_blocks for part in pair]
+    dy_pieces = [part for pair in dy_blocks for part in pair]
+
+    saved = forward_rows(x_pieces, gate_weight[0], up_weight[0], lower_cat, upper_tiles)
+    weights = (gate_weight[0], up_weight[0], down_weight[0])
+    sums, parts, owned = [], [], []
+    chips = SHARDS // 2
+    rows = 2 * tokens_each
+    for chip in range(chips):
+        keep, away, part, own = backward_rows(
+            dy_pieces[4 * chip : 4 * chip + 4],
+            chip * rows,
+            route_column[chip * rows : chip * rows + rows],
+            weights,
+            down_upper,
+            down_lower,
+            gate_upper,
+            up_upper,
+            saved,
+        )
+        sums.append((keep, swap(away, CORE)))
+        parts.append(part)
+        owned.append(own)
+
+    half = experts // 2
+    lo, hi = slice(0, half), slice(half, experts)
+    (own_a, own_b), (across_a, across_b), (along_a, along_b), (far_a, far_b) = sums
+    far_lo = swap(added(far_a[lo], far_b[lo]), ACROSS)
+    far_hi = swap(added(far_a[hi], far_b[hi]), ALONG)
+    got_across_lo = swap(added(across_a[lo], across_b[lo]), ACROSS)
+    got_along_hi = swap(added(along_a[hi], along_b[hi]), ALONG)
+    got_across_hi = swap(added(added(across_a[hi], across_b[hi]), far_hi), ACROSS)
+    got_along_lo = swap(added(added(along_a[lo], along_b[lo]), far_lo), ALONG)
+
+    total = jnp.stack(parts, axis=0).reshape(chips, 3 * rank, 2, tokens_each)
+    total = total.transpose(0, 2, 1, 3)
+    for bit in (CORE, ACROSS, ALONG):
+        other = swap(total.reshape(SHARDS, 3 * rank, tokens_each), bit)
+        shape = (SHARDS // (2 * bit), 2, bit, 3 * rank, tokens_each)
+        total = total.reshape(shape) + other.reshape(shape)[:, ::-1]
+    total = total.reshape(SHARDS, 3 * rank, tokens_each)
+    lower_slabs = lower_cat.reshape(2 * rank, experts, feat).transpose(1, 0, 2)
+    low_rows = ADAPTER_SCALE * lax.dot_general(
+        jnp.broadcast_to(total[0, : 2 * rank].astype(jnp.bfloat16), (experts, 2 * rank, tokens_each)),
+        lower_slabs,
+        (((1,), (1,)), ((0,), (0,))),
+        preferred_element_type=jnp.float32,
+    )
+
+    def wide(value):
+        return value.astype(jnp.float32)
+
+    from_neighbours = jnp.concatenate(
+        [wide(got_across_lo) + wide(got_along_lo), wide(got_across_hi) + wide(got_along_hi)], axis=0
+    )
+    rows_sum = (wide(own_a) + wide(own_b) + from_neighbours + low_rows).astype(jnp.bfloat16)
+    grad_x = lax.psum_scatter(rows_sum, "expert", scatter_dimension=0, tiled=True)[0]
+
+    grad_pair, grad_down = shared_gradients(
+        x_pieces,
+        dy_pieces,
+        order,
+        total[:, : 2 * rank],
+        total[:, 2 * rank :] * route[:, None, :],
+    )
+    owned_sum = sum(owned[1:], owned[0])
+    return (
+        grad_x,
+        grad_pair[None, :rank],
+        owned_sum[0].T[None],
+        grad_pair[None, rank:],
+        owned_sum[1].T[None],
+        owned_sum[2][None],
+        grad_down.T[None],
+    )
+
+
+def plan(tokens, *others):
+    planned = (
+        lax.axis_size("dp") == SHARDS
+        and lax.axis_size("expert") % 2 == 0
+        and others[3].shape[1] % LANES == 0
+        and tokens.shape[0] % LANES == 0
+    )
+    return (local if planned else general_local)(tokens, *others)
+
+
 def solution(mesh):
     return jax.shard_map(
-        local,
+        plan,
         mesh=mesh,
         in_specs=(
             P("dp", "expert"),

time: 445 us -> 327 us (0.73); the launches traced: 436 us -> 326 us
  matrix products: 135 us -> 1.62 us
  Pallas kernels: 0 us -> 131 us
  waiting for transfers between devices: 188 us -> 107 us
  blocking collectives: 60 us -> 15.4 us
  starting transfers between devices: 4.72 us -> 27.1 us
  local copies, waits for them, and re-layouts: 24.8 us -> 18.5 us
    dot_general x20 -> x1, matrix products: 135 us -> 1.62 us  [local(): lax.dot_general(jnp.broadcast_to(total[0, :2 * rank].astype(jnp.bfloat16)...]
    pallas_call x0 -> x6, Pallas kernels: none -> 131 us  [the longest x4 85.9 us: backward_rows(): pl.pallas_call(lambda *refs: backward_kernel(len(pieces), row_start, *ref...]
    ppermute x0 -> x41, waiting for transfers between devices: none -> 64.3 us  [swap(): return lax.ppermute(value, 'dp', [(i, i ^ bit) for i in range(SHARDS)])]
    all_to_all x2 -> x0, blocking collectives: 60 us -> none  [the longest x1 31.9 us: local(): lax.all_to_all(send_dy, 'expert', split_axis=0, concat_axis=2, tiled=True)]
    reduce_scatter x1, waiting for transfers between devices: 64.2 us -> 10.1 us  [local(): lax.psum_scatter(rows_sum, 'expert', scatter_dimension=0, tiled=True)[0]]
    psum x1 -> x0, waiting for transfers between devices: 49.3 us -> none  [local(): lax.psum(shared_slice[0].astype(jnp.bfloat16), 'dp').astype(jnp.float32)]
    all_gather x2, waiting for transfers between devices: 74.4 us -> 31.5 us  [the longest x1 31.5 us: local(): x_here = lax.all_gather(tokens, 'expert', axis=0, tiled=False)]
    ppermute x0 -> x41, starting transfers between devices: none -> 27 us  [swap(): return lax.ppermute(value, 'dp', [(i, i ^ bit) for i in range(SHARDS)])]
  transfers between devices with their start and end apart: 5 -> 44, of which waited for: 4 -> 11; matrix products, arithmetic and copies ran while one was open for 9% -> 7% of each run, Pallas kernels for 0% -> 40%
where the time goes in v1:
time: 327 us; the launch traced here: 326 us
  Pallas kernels  131 us (40%)
  waiting for transfers between devices  107 us (33%)
  starting transfers between devices  27.1 us (8%)
  local copies, waits for them, and re-layouts  18.5 us (6%)
  blocking collectives  15.4 us (5%)
  between operations  14.4 us (4%)
  other arithmetic  10.2 us (3%)
    pallas_call x4, Pallas kernels, backward_rows(): pl.pallas_call(lambda *refs: backward_kernel(len(pieces), row_start, *ref...  85.9 us
    ppermute x41, waiting for transfers between devices, swap(): return lax.ppermute(value, 'dp', [(i, i ^ bit) for i in range(SHARDS)])  64.3 us
    pallas_call x1, Pallas kernels, forward_rows(): pl.pallas_call(lambda *refs: forward_kernel(len(pieces), *refs), out_shap...  33.8 us
    all_gather x1, waiting for transfers between devices, local(): x_here = lax.all_gather(tokens, 'expert', axis=0, tiled=False)  31.5 us
    ppermute x41, starting transfers between devices, swap(): return lax.ppermute(value, 'dp', [(i, i ^ bit) for i in range(SHARDS)])  27 us
    all_gather x1, blocking collectives, local(): all_routes = lax.all_gather(weight_of.T, 'dp', axis=0, tiled=False)  15.4 us
    pallas_call x1, Pallas kernels, shared_gradients(): pl.pallas_call(lambda *refs: shared_kernel(n_pieces, *refs), out_shape=(j...  11.7 us
    reduce_scatter x1, waiting for transfers between devices, local(): lax.psum_scatter(rows_sum, 'expert', scatter_dimension=0, tiled=True)[0]  10.1 us
  transfers between devices with their start and end apart: 44, of which 11 were waited for; matrix products, arithmetic and copies ran while one was open for 7% of the time, Pallas kernels for 40%

profile of v1, /device:TPU:0, one launch (start us, length us, event | category | flops | bytes accessed | tf_op | source)
XLA Modules:
  0.0 326.0 jit_solution(9306165287233299398)
XLA Ops:
  8.8 31.5 %all-gather.9.cloned.1.call-done = bf16[512,1024]{1,0:T(8,128)(2,1)} async-done(((bf16[128,1024]{1,0:T(8,128)(2,1)}), bf16[512,1024]{1,0:T(8,128)(2,1)}) %all-gather.9.cloned.1.call-update) | async-done | bytes 1048592 | tf_op jit(solution)/shard_map/all_gather | solution.py:636
  40.3 1.3 fusion.16
  41.5 1.5 collective-permute-start
  43.6 1.5 collective-permute-start.2
  45.7 10.8 %collective-permute-done.refs_4_ = bf16[2,128,1024]{2,1,0:T(8,128)(2,1)S(1)} collective-permute-done((bf16[2,128,1024]{2,1,0:T(8,128)(2,1)S(1)}, bf16[2,128,1024]{2,1,0:T(8,128)(2,1)S(1)}, u32[]{:S(2)}, u32[]{:S(2)}) %collective-permute-start) | collective-permute-done | bytes 524320 | tf_op jit(solution)/shard_map/ppermute | solution.py:573
  56.5 15.4 %all-gather.3 = f32[8,4,128]{2,1,0:T(4,128)S(1)} all-gather(f32[1,4,128]{2,1,0:T(4,128)S(1)} %bitcast.135), channel_id=4, replica_groups=mesh['dp'=8,'expert'=4] {'dp'}, dimensions={0}, use_global_device_ids=true | all-gather | bytes 18432 | tf_op jit(solution)/shard_map/all_gather | solution.py:619
  71.9 0.9 copy-done.25
  72.8 1.3 fusion.15
  74.1 1.5 collective-permute-start.23
  76.7 1.5 collective-permute-start.13
  79.6 0.8 copy.57.refs_4_
  80.4 0.8 copy.56.refs_4_
  82.0 6.9 %collective-permute-done.23.refs_0_.refs_24_ = bf16[2,128,1024]{2,1,0:T(8,128)(2,1)S(1)} collective-permute-done((bf16[2,128,1024]{2,1,0:T(8,128)(2,1)S(1)}, bf16[2,128,1024]{2,1,0:T(8,128)(2,1)S(1)}, u32[]{:S(2)}, u32[]{:S(2)}) %collective-permute-start.23) | collective-permute-done | bytes 524320 | tf_op jit(solution)/shard_map/ppermute | solution.py:573
  88.9 1.5 collective-permute-start.24
  91.0 9.3 %collective-permute-done.13.refs_13_ = bf16[2,128,1024]{2,1,0:T(8,128)(2,1)} collective-permute-done((bf16[2,128,1024]{2,1,0:T(8,128)(2,1)}, bf16[2,128,1024]{2,1,0:T(8,128)(2,1)}, u32[]{:S(2)}, u32[]{:S(2)}) %collective-permute-start.13) | collective-permute-done | bytes 524320 | tf_op jit(solution)/shard_map/ppermute | solution.py:573
  101.7 1.5 collective-permute-start.18
  103.7 7.1 %collective-permute-done.24.refs_1_.refs_25_ = bf16[2,128,1024]{2,1,0:T(8,128)(2,1)S(1)} collective-permute-done((bf16[2,128,1024]{2,1,0:T(8,128)(2,1)S(1)}, bf16[2,128,1024]{2,1,0:T(8,128)(2,1)S(1)}, u32[]{:S(2)}, u32[]{:S(2)}) %collective-permute-start.24) | collective-permute-done | bytes 524320 | tf_op jit(solution)/shard_map/ppermute | solution.py:573
  111.3 0.8 copy-done.27
  112.2 33.8 %forward_rows.1 = (f32[1024,896]{1,0:T(8,128)}, f32[1024,896]{1,0:T(8,128)}, bf16[1024,896]{1,0:T(8,128)(2,1)}, bf16[1024,32]{1,0:T(8,128)(2,1)}) custom-call(bf16[2,128,1024]{2,1,0:T(8,128)(2,1)} %bitcast.107, bf16[2,128,1024]{2,1,0:T(8,128)(2,1)} %bitcast.102, bf16[2,128,1024]{2,1,0:T(8,128)(2,1)} %collective-permute-done.6.refs_2_, ...), custom_call_target="tpu_custom_call" | custom-call | flops 15032385536 | bytes 40000000 | tf_op jit(solution)/shard_map/forward_rows/pallas_call | solution.py:294
  146.0 1.5 collective-permute-start.28
  149.2 21.4 %backward_rows.6 = (bf16[4,128,1024]{2,1,0:T(8,128)(2,1)}, bf16[4,128,1024]{2,1,0:T(8,128)(2,1)}, f32[48,256]{1,0:T(8,128)}, f32[3,16,896]{2,1,0:T(8,128)}) custom-call(bf16[2,128,1024]{2,1,0:T(8,128)(2,1)} %copy-done.2, bf16[2,128,1024]{2,1,0:T(8,128)(2,1)} %copy-done.3, bf16[2,128,1024]{2,1,0:T(8,128)(2,1)} %copy-done.7, bf16[2,128,1024]{2,1,0:T(8,128)(2,1)} %copy-done.8, ...), custom_call_target="tpu_custom_call" | custom-call | flops 5637144576 | bytes 26214400 | tf_op jit(solution)/shard_map/backward_rows/pallas_call | solution.py:460
  172.0 21.4 %backward_rows.5 = (bf16[4,128,1024]{2,1,0:T(8,128)(2,1)}, bf16[4,128,1024]{2,1,0:T(8,128)(2,1)}, f32[48,256]{1,0:T(8,128)}, f32[3,16,896]{2,1,0:T(8,128)}) custom-call(bf16[2,128,1024]{2,1,0:T(8,128)(2,1)} %copy-done.5, bf16[2,128,1024]{2,1,0:T(8,128)(2,1)} %copy-done.4, bf16[2,128,1024]{2,1,0:T(8,128)(2,1)} %copy-done.11, ...), custom_call_target="tpu_custom_call" | custom-call | flops 5637144576 | bytes 26214400 | tf_op jit(solution)/shard_map/backward_rows/pallas_call | solution.py:460
  194.3 0.8 copy-done.14
  195.1 21.4 %backward_rows.7 = (bf16[4,128,1024]{2,1,0:T(8,128)(2,1)}, bf16[4,128,1024]{2,1,0:T(8,128)(2,1)}, f32[48,256]{1,0:T(8,128)}, f32[3,16,896]{2,1,0:T(8,128)}) custom-call(bf16[2,128,1024]{2,1,0:T(8,128)(2,1)} %copy-done.9, bf16[2,128,1024]{2,1,0:T(8,128)(2,1)} %copy-done.10, bf16[2,128,1024]{2,1,0:T(8,128)(2,1)} %copy-done.13, ...), custom_call_target="tpu_custom_call" | custom-call | flops 5637144576 | bytes 26214400 | tf_op jit(solution)/shard_map/backward_rows/pallas_call | solution.py:460
  217.8 0.8 copy-done.12
  218.6 21.6 %backward_rows.4 = (bf16[4,128,1024]{2,1,0:T(8,128)(2,1)}, bf16[4,128,1024]{2,1,0:T(8,128)(2,1)}, f32[48,256]{1,0:T(8,128)}, f32[3,16,896]{2,1,0:T(8,128)}) custom-call(bf16[2,128,1024]{2,1,0:T(8,128)(2,1)} %copy-done.1, bf16[2,128,1024]{2,1,0:T(8,128)(2,1)} %copy-done, bf16[2,128,1024]{2,1,0:T(8,128)(2,1)} %copy-done.6, bf16[2,128,1024]{2,1,0:T(8,128)(2,1)} %copy-done.12, ...), custom_call_target="tpu_custom_call" | custom-call | flops 5637144576 | bytes 26214400 | tf_op jit(solution)/shard_map/backward_rows/pallas_call | solution.py:460
  240.3 0.8 stack.15
  241.5 1.7 add_convert_fusion.5
  243.2 1.5 collective-permute-start.33
  245.4 1.5 collective-permute-start.35
  246.8 14.8 %collective-permute-done.39 = f32[8,48,128]{2,1,0:T(8,128)S(1)} collective-permute-done((f32[8,48,128]{2,1,0:T(8,128)S(1)}, f32[8,48,128]{2,1,0:T(8,128)S(1)}, u32[]{:S(2)}, u32[]{:S(2)}) %collective-permute-start.39) | collective-permute-done | bytes 196640 | tf_op jit(solution)/shard_map/ppermute | solution.py:573
  261.7 1.5 collective-permute-start.40
  263.2 1.7 add_convert_fusion.4
  265.6 1.7 add_convert_fusion.7
  267.3 1.5 collective-permute-start.36
  269.5 1.0 concatenate.28
  270.5 0.9 copy.64
  272.1 1.5 collective-permute-start.22
  273.6 0.9 reverse_add_fusion
  274.6 6.0 %collective-permute-done.37 = bf16[2,128,1024]{2,1,0:T(8,128)(2,1)} collective-permute-done((bf16[2,128,1024]{2,1,0:T(8,128)(2,1)S(1)}, bf16[2,128,1024]{2,1,0:T(8,128)(2,1)}, u32[]{:S(2)}, u32[]{:S(2)}) %collective-permute-start.37) | collective-permute-done | bytes 524320 | tf_op jit(solution)/shard_map/ppermute | solution.py:573
  280.6 1.7 collective-permute-done.36
  282.3 1.4 convert_add_fusion
  283.7 6.9 %collective-permute-done.34 = bf16[2,128,1024]{2,1,0:T(8,128)(2,1)S(1)} collective-permute-done((bf16[2,128,1024]{2,1,0:T(8,128)(2,1)S(1)}, bf16[2,128,1024]{2,1,0:T(8,128)(2,1)S(1)}, u32[]{:S(2)}, u32[]{:S(2)}) %collective-permute-start.34) | collective-permute-done | bytes 524320 | tf_op jit(solution)/shard_map/ppermute | solution.py:573
  290.5 0.8 collective-permute-done.22
  291.6 1.6 fusion.1
  295.8 11.7 %shared_gradients.1 = (f32[32,4096]{1,0:T(8,128)}, f32[16,4096]{1,0:T(8,128)}) custom-call(bf16[2,128,1024]{2,1,0:T(8,128)(2,1)} %bitcast.108, bf16[2,128,1024]{2,1,0:T(8,128)(2,1)} %bitcast.103, bf16[2,128,1024]{2,1,0:T(8,128)(2,1)} %collective-permute-done.6.refs_2_, bf16[2,128,1024]{2,1,0:T(8,128)(2,1)} %collective-permute-done.7.refs_3_, ...), custom_call_target="tpu_custom_call" | custom-call | flops 2147483648 | bytes 16777216 | tf_op jit(solution)/shard_map/shared_gradients/pallas_call | solution.py:546
  307.4 1.9 slice_bitcast_fusion
  309.3 10.1 %reduce-scatter.2.cloned.1.call-done = bf16[1,128,1024]{2,1,0:T(8,128)(2,1)} async-done(((bf16[4,128,1024]{2,1,0:T(8,128)(2,1)}), bf16[1,128,1024]{2,1,0:T(8,128)(2,1)}) %reduce-scatter.2.cloned.1.call-update) | async-done | bytes 262160 | tf_op jit(solution)/shard_map/reduce_scatter | solution.py:699
  (173 shorter events, 19.9 us)
Async XLA Ops:
  7.2 33.1 %all-gather.9.cloned.1.call-start = ((), (), s32[]{:S(2)}) async-start(), calls=%async_computation.3 | async-start | bytes 1310720 | tf_op jit(solution)/shard_map/all_gather | solution.py:636
  7.9 64.0 %all-gather.7.cloned.1.call-start = ((), (), s32[]{:S(2)}) async-start(), calls=%async_computation.2 | async-start | bytes 1310720 | tf_op jit(solution)/shard_map/all_gather | solution.py:637
  8.7 73.3 %copy-start.21 = (bf16[1,896,16]{1,2,0:T(8,128)(2,1)S(1)}, bf16[1,896,16]{1,2,0:T(8,128)(2,1)}, u32[]{:S(2)}) copy-start(bf16[1,896,16]{1,2,0:T(8,128)(2,1)} %param.21) | copy-start | bytes 86020
  8.7 92.2 %copy-start.28 = (bf16[1,16,4096]{2,1,0:T(8,128)(2,1)S(1)}, bf16[1,16,4096]{2,1,0:T(8,128)(2,1)}, u32[]{:S(2)}) copy-start(bf16[1,16,4096]{2,1,0:T(8,128)(2,1)} %param.22) | copy-start | bytes 393220
  8.7 92.2 %copy-start.30 = (bf16[1,16,4096]{2,1,0:T(8,128)(2,1)S(1)}, bf16[1,16,4096]{2,1,0:T(8,128)(2,1)}, u32[]{:S(2)}) copy-start(bf16[1,16,4096]{2,1,0:T(8,128)(2,1)} %param.20) | copy-start | bytes 393220
  8.7 310.7 %reduce-scatter.2.cloned.1.call-start = ((), (), s32[]{:S(2)}) async-start(), calls=%async_computation.1 | async-start | bytes 1310720 | tf_op jit(solution)/shard_map/reduce_scatter | solution.py:699
  41.5 14.9 %collective-permute-start = (bf16[2,128,1024]{2,1,0:T(8,128)(2,1)S(1)}, bf16[2,128,1024]{2,1,0:T(8,128)(2,1)S(1)}, u32[]{:S(2)}, u32[]{:S(2)}) collective-permute-start(bf16[2,128,1024]{2,1,0:T(8,128)(2,1)S(1)} %bitcast.104), channel_id=1, source_target_pairs={{0,8},{4,12},{8,0},{12,4},{16,24},{20,28},{24,16},{28,20},{1,9},{5... | collective-permute-start | bytes 1572872 | tf_op jit(solution)/shard_map/ppermute | solution.py:573
  43.1 28.8 %collective-permute-start.1 = (bf16[2,128,1024]{2,1,0:T(8,128)(2,1)S(1)}, bf16[2,128,1024]{2,1,0:T(8,128)(2,1)S(1)}, u32[]{:S(2)}, u32[]{:S(2)}) collective-permute-start(bf16[2,128,1024]{2,1,0:T(8,128)(2,1)S(1)} %bitcast.99), channel_id=1, source_target_pairs={{0,8},{4,12},{8,0},{12,4},{16,24},{20,28},{24,16},{28,20},{1,9},{5... | collective-permute-start | bytes 1572872 | tf_op jit(solution)/shard_map/ppermute | solution.py:573
  43.6 28.3 %collective-permute-start.2 = (bf16[2,128,1024]{2,1,0:T(8,128)(2,1)S(1)}, bf16[2,128,1024]{2,1,0:T(8,128)(2,1)}, u32[]{:S(2)}, u32[]{:S(2)}) collective-permute-start(bf16[2,128,1024]{2,1,0:T(8,128)(2,1)S(1)} %bitcast.105), channel_id=1, source_target_pairs={{0,16},{4,20},{8,24},{12,28},{16,0},{20,4},{24,8},{28,12},{1,17},{... | collective-permute-start | bytes 1572872 | tf_op jit(solution)/shard_map/ppermute | solution.py:573
  45.1 26.8 %collective-permute-start.3 = (bf16[2,128,1024]{2,1,0:T(8,128)(2,1)S(1)}, bf16[2,128,1024]{2,1,0:T(8,128)(2,1)S(1)}, u32[]{:S(2)}, u32[]{:S(2)}) collective-permute-start(bf16[2,128,1024]{2,1,0:T(8,128)(2,1)S(1)} %bitcast.100), channel_id=1, source_target_pairs={{0,16},{4,20},{8,24},{12,28},{16,0},{20,4},{24,8},{28,12},{1,17},{... | collective-permute-start | bytes 1572872 | tf_op jit(solution)/shard_map/ppermute | solution.py:573
  45.7 30.5 %collective-permute-start.6 = (bf16[2,128,1024]{2,1,0:T(8,128)(2,1)S(1)}, bf16[2,128,1024]{2,1,0:T(8,128)(2,1)}, u32[]{:S(2)}, u32[]{:S(2)}) collective-permute-start(bf16[2,128,1024]{2,1,0:T(8,128)(2,1)S(1)} %bitcast.106), channel_id=1, source_target_pairs={{0,4},{4,0},{8,12},{12,8},{16,20},{20,16},{24,28},{28,24},{1,5},{5... | collective-permute-start | bytes 1572872 | tf_op jit(solution)/shard_map/ppermute | solution.py:573
  56.4 20.3 %collective-permute-start.7 = (bf16[2,128,1024]{2,1,0:T(8,128)(2,1)S(1)}, bf16[2,128,1024]{2,1,0:T(8,128)(2,1)}, u32[]{:S(2)}, u32[]{:S(2)}) collective-permute-start(bf16[2,128,1024]{2,1,0:T(8,128)(2,1)S(1)} %bitcast.101), channel_id=1, source_target_pairs={{0,4},{4,0},{8,12},{12,8},{16,20},{20,16},{24,28},{28,24},{1,5},{5... | collective-permute-start | bytes 1572872 | tf_op jit(solution)/shard_map/ppermute | solution.py:573
  74.1 96.5 %copy-start = (bf16[2,128,1024]{2,1,0:T(8,128)(2,1)}, bf16[2,128,1024]{2,1,0:T(8,128)(2,1)S(1)}, u32[]{:S(2)}) copy-start(bf16[2,128,1024]{2,1,0:T(8,128)(2,1)S(1)} %get-tuple-element.67.refs_1_.refs_17_) | copy-start | bytes 1572868
  74.1 14.8 %collective-permute-start.23 = (bf16[2,128,1024]{2,1,0:T(8,128)(2,1)S(1)}, bf16[2,128,1024]{2,1,0:T(8,128)(2,1)S(1)}, u32[]{:S(2)}, u32[]{:S(2)}) collective-permute-start(bf16[2,128,1024]{2,1,0:T(8,128)(2,1)S(1)} %get-tuple-element.68.refs_0_.refs_16_), channel_id=1, source_target_pairs={{0,16},{4,20},{8,24},{12,28},{16,0},{20,4},{24,8},{28,12},{1,17},{... | collective-permute-start | bytes 1572872 | tf_op jit(solution)/shard_map/ppermute | solution.py:573
  75.6 14.8 %collective-permute-start.8 = (bf16[2,128,1024]{2,1,0:T(8,128)(2,1)S(1)}, bf16[2,128,1024]{2,1,0:T(8,128)(2,1)}, u32[]{:S(2)}, u32[]{:S(2)}) collective-permute-start(bf16[2,128,1024]{2,1,0:T(8,128)(2,1)S(1)} %collective-permute-done.refs_4_), channel_id=1, source_target_pairs={{0,4},{4,0},{8,12},{12,8},{16,20},{20,16},{24,28},{28,24},{1,5},{5... | collective-permute-start | bytes 1572872 | tf_op jit(solution)/shard_map/ppermute | solution.py:573
  75.7 14.7 %collective-permute-start.9 = (bf16[2,128,1024]{2,1,0:T(8,128)(2,1)}, bf16[2,128,1024]{2,1,0:T(8,128)(2,1)}, u32[]{:S(2)}, u32[]{:S(2)}) collective-permute-start(bf16[2,128,1024]{2,1,0:T(8,128)(2,1)} %copy-done.24), channel_id=1, source_target_pairs={{0,4},{4,0},{8,12},{12,8},{16,20},{20,16},{24,28},{28,24},{1,5},{5... | collective-permute-start | bytes 1572872 | tf_op jit(solution)/shard_map/ppermute | solution.py:573
  76.2 14.8 %collective-permute-start.12 = (bf16[2,128,1024]{2,1,0:T(8,128)(2,1)}, bf16[2,128,1024]{2,1,0:T(8,128)(2,1)}, u32[]{:S(2)}, u32[]{:S(2)}) collective-permute-start(bf16[2,128,1024]{2,1,0:T(8,128)(2,1)} %collective-permute-done.2.refs_8_), channel_id=1, source_target_pairs={{0,8},{4,12},{8,0},{12,4},{16,24},{20,28},{24,16},{28,20},{1,9},{5... | collective-permute-start | bytes 1572872 | tf_op jit(solution)/shard_map/ppermute | solution.py:573
  76.7 23.5 %collective-permute-start.13 = (bf16[2,128,1024]{2,1,0:T(8,128)(2,1)}, bf16[2,128,1024]{2,1,0:T(8,128)(2,1)}, u32[]{:S(2)}, u32[]{:S(2)}) collective-permute-start(bf16[2,128,1024]{2,1,0:T(8,128)(2,1)} %copy-done.24), channel_id=1, source_target_pairs={{0,16},{4,20},{8,24},{12,28},{16,0},{20,4},{24,8},{28,12},{1,17},{... | collective-permute-start | bytes 1572872 | tf_op jit(solution)/shard_map/ppermute | solution.py:573
  88.9 21.9 %collective-permute-start.24 = (bf16[2,128,1024]{2,1,0:T(8,128)(2,1)S(1)}, bf16[2,128,1024]{2,1,0:T(8,128)(2,1)S(1)}, u32[]{:S(2)}, u32[]{:S(2)}) collective-permute-start(bf16[2,128,1024]{2,1,0:T(8,128)(2,1)S(1)} %get-tuple-element.67.refs_1_.refs_17_), channel_id=1, source_target_pairs={{0,16},{4,20},{8,24},{12,28},{16,0},{20,4},{24,8},{28,12},{1,17},{... | collective-permute-start | bytes 1572872 | tf_op jit(solution)/shard_map/ppermute | solution.py:573
  90.4 11.3 %collective-permute-start.10 = (bf16[2,128,1024]{2,1,0:T(8,128)(2,1)}, bf16[2,128,1024]{2,1,0:T(8,128)(2,1)S(1)}, u32[]{:S(2)}, u32[]{:S(2)}) collective-permute-start(bf16[2,128,1024]{2,1,0:T(8,128)(2,1)} %collective-permute-done.2.refs_8_), channel_id=1, source_target_pairs={{0,4},{4,0},{8,12},{12,8},{16,20},{20,16},{24,28},{28,24},{1,5},{5... | collective-permute-start | bytes 1572872 | tf_op jit(solution)/shard_map/ppermute | solution.py:573
  90.4 12.8 %collective-permute-start.11 = (bf16[2,128,1024]{2,1,0:T(8,128)(2,1)}, bf16[2,128,1024]{2,1,0:T(8,128)(2,1)}, u32[]{:S(2)}, u32[]{:S(2)}) collective-permute-start(bf16[2,128,1024]{2,1,0:T(8,128)(2,1)} %copy-done.25), channel_id=1, source_target_pairs={{0,4},{4,0},{8,12},{12,8},{16,20},{20,16},{24,28},{28,24},{1,5},{5... | collective-permute-start | bytes 1572872 | tf_op jit(solution)/shard_map/ppermute | solution.py:573
  90.9 19.9 %collective-permute-start.14 = (bf16[2,128,1024]{2,1,0:T(8,128)(2,1)}, bf16[2,128,1024]{2,1,0:T(8,128)(2,1)}, u32[]{:S(2)}, u32[]{:S(2)}) collective-permute-start(bf16[2,128,1024]{2,1,0:T(8,128)(2,1)} %collective-permute-done.12.refs_12_), channel_id=1, source_target_pairs={{0,4},{4,0},{8,12},{12,8},{16,20},{20,16},{24,28},{28,24},{1,5},{5... | collective-permute-start | bytes 1572872 | tf_op jit(solution)/shard_map/ppermute | solution.py:573
  100.3 11.1 %collective-permute-start.15 = (bf16[2,128,1024]{2,1,0:T(8,128)(2,1)}, bf16[2,128,1024]{2,1,0:T(8,128)(2,1)S(1)}, u32[]{:S(2)}, u32[]{:S(2)}) collective-permute-start(bf16[2,128,1024]{2,1,0:T(8,128)(2,1)} %collective-permute-done.13.refs_13_), channel_id=1, source_target_pairs={{0,4},{4,0},{8,12},{12,8},{16,20},{20,16},{24,28},{28,24},{1,5},{5... | collective-permute-start | bytes 1572872 | tf_op jit(solution)/shard_map/ppermute | solution.py:573
  101.7 44.4 %collective-permute-start.18 = (bf16[2,128,1024]{2,1,0:T(8,128)(2,1)S(1)}, bf16[2,128,1024]{2,1,0:T(8,128)(2,1)S(1)}, u32[]{:S(2)}, u32[]{:S(2)}) collective-permute-start(bf16[2,128,1024]{2,1,0:T(8,128)(2,1)S(1)} %get-tuple-element.67.refs_1_.refs_17_), channel_id=1, source_target_pairs={{0,8},{4,12},{8,0},{12,4},{16,24},{20,28},{24,16},{28,20},{1,9},{5... | collective-permute-start | bytes 1572872 | tf_op jit(solution)/shard_map/ppermute | solution.py:573
  103.2 44.4 %collective-permute-start.17 = (bf16[2,128,1024]{2,1,0:T(8,128)(2,1)S(1)}, bf16[2,128,1024]{2,1,0:T(8,128)(2,1)S(1)}, u32[]{:S(2)}, u32[]{:S(2)}) collective-permute-start(bf16[2,128,1024]{2,1,0:T(8,128)(2,1)S(1)} %get-tuple-element.68.refs_0_.refs_16_), channel_id=1, source_target_pairs={{0,8},{4,12},{8,0},{12,4},{16,24},{20,28},{24,16},{28,20},{1,9},{5... | collective-permute-start | bytes 1572872 | tf_op jit(solution)/shard_map/ppermute | solution.py:573
  110.8 106.2 %collective-permute-start.4 = (bf16[2,128,1024]{2,1,0:T(8,128)(2,1)S(1)}, bf16[2,128,1024]{2,1,0:T(8,128)(2,1)S(1)}, u32[]{:S(2)}, u32[]{:S(2)}) collective-permute-start(bf16[2,128,1024]{2,1,0:T(8,128)(2,1)S(1)} %get-tuple-element.68.refs_0_.refs_16_), channel_id=1, source_target_pairs={{0,4},{4,0},{8,12},{12,8},{16,20},{20,16},{24,28},{28,24},{1,5},{5... | collective-permute-start | bytes 1572872 | tf_op jit(solution)/shard_map/ppermute | solution.py:573
  110.8 37.3 %collective-permute-start.25 = (bf16[2,128,1024]{2,1,0:T(8,128)(2,1)S(1)}, bf16[2,128,1024]{2,1,0:T(8,128)(2,1)S(1)}, u32[]{:S(2)}, u32[]{:S(2)}) collective-permute-start(bf16[2,128,1024]{2,1,0:T(8,128)(2,1)S(1)} %collective-permute-done.23.refs_0_.refs_24_), channel_id=1, source_target_pairs={{0,4},{4,0},{8,12},{12,8},{16,20},{20,16},{24,28},{28,24},{1,5},{5... | collective-permute-start | bytes 1572872 | tf_op jit(solution)/shard_map/ppermute | solution.py:573
  112.1 36.0 %collective-permute-start.26 = (bf16[2,128,1024]{2,1,0:T(8,128)(2,1)S(1)}, bf16[2,128,1024]{2,1,0:T(8,128)(2,1)S(1)}, u32[]{:S(2)}, u32[]{:S(2)}) collective-permute-start(bf16[2,128,1024]{2,1,0:T(8,128)(2,1)S(1)} %collective-permute-done.24.refs_1_.refs_25_), channel_id=1, source_target_pairs={{0,4},{4,0},{8,12},{12,8},{16,20},{20,16},{24,28},{28,24},{1,5},{5... | collective-permute-start | bytes 1572872 | tf_op jit(solution)/shard_map/ppermute | solution.py:573
  146.0 24.5 %collective-permute-start.28 = (bf16[2,128,1024]{2,1,0:T(8,128)(2,1)S(1)}, bf16[2,128,1024]{2,1,0:T(8,128)(2,1)S(1)}, u32[]{:S(2)}, u32[]{:S(2)}) collective-permute-start(bf16[2,128,1024]{2,1,0:T(8,128)(2,1)S(1)} %collective-permute-done.23.refs_0_.refs_24_), channel_id=1, source_target_pairs={{0,8},{4,12},{8,0},{12,4},{16,24},{20,28},{24,16},{28,20},{1,9},{5... | collective-permute-start | bytes 1572872 | tf_op jit(solution)/shard_map/ppermute | solution.py:573
  147.6 23.5 %collective-permute-start.29 = (bf16[2,128,1024]{2,1,0:T(8,128)(2,1)S(1)}, bf16[2,128,1024]{2,1,0:T(8,128)(2,1)S(1)}, u32[]{:S(2)}, u32[]{:S(2)}) collective-permute-start(bf16[2,128,1024]{2,1,0:T(8,128)(2,1)S(1)} %collective-permute-done.18.refs_1_.refs_21_), channel_id=1, source_target_pairs={{0,16},{4,20},{8,24},{12,28},{16,0},{20,4},{24,8},{28,12},{1,17},{... | collective-permute-start | bytes 1572872 | tf_op jit(solution)/shard_map/ppermute | solution.py:573
  148.2 23.4 %collective-permute-start.20 = (bf16[2,128,1024]{2,1,0:T(8,128)(2,1)S(1)}, bf16[2,128,1024]{2,1,0:T(8,128)(2,1)}, u32[]{:S(2)}, u32[]{:S(2)}) collective-permute-start(bf16[2,128,1024]{2,1,0:T(8,128)(2,1)S(1)} %collective-permute-done.18.refs_1_.refs_21_), channel_id=1, source_target_pairs={{0,4},{4,0},{8,12},{12,8},{16,20},{20,16},{24,28},{28,24},{1,5},{5... | collective-permute-start | bytes 1572872 | tf_op jit(solution)/shard_map/ppermute | solution.py:573
  148.2 23.0 %collective-permute-start.19 = (bf16[2,128,1024]{2,1,0:T(8,128)(2,1)S(1)}, bf16[2,128,1024]{2,1,0:T(8,128)(2,1)S(1)}, u32[]{:S(2)}, u32[]{:S(2)}) collective-permute-start(bf16[2,128,1024]{2,1,0:T(8,128)(2,1)S(1)} %collective-permute-done.17.refs_0_.refs_20_), channel_id=1, source_target_pairs={{0,4},{4,0},{8,12},{12,8},{16,20},{20,16},{24,28},{28,24},{1,5},{5... | collective-permute-start | bytes 1572872 | tf_op jit(solution)/shard_map/ppermute | solution.py:573
  170.6 46.4 %collective-permute-start.5 = (bf16[2,128,1024]{2,1,0:T(8,128)(2,1)S(1)}, bf16[2,128,1024]{2,1,0:T(8,128)(2,1)S(1)}, u32[]{:S(2)}, u32[]{:S(2)}) collective-permute-start(bf16[2,128,1024]{2,1,0:T(8,128)(2,1)S(1)} %get-tuple-element.67.refs_1_.refs_17_), channel_id=1, source_target_pairs={{0,4},{4,0},{8,12},{12,8},{16,20},{20,16},{24,28},{28,24},{1,5},{5... | collective-permute-start | bytes 1572872 | tf_op jit(solution)/shard_map/ppermute | solution.py:573
  171.0 92.1 %collective-permute-start.27 = (bf16[4,128,1024]{2,1,0:T(8,128)(2,1)}, bf16[4,128,1024]{2,1,0:T(8,128)(2,1)}, u32[]{:S(2)}, u32[]{:S(2)}) collective-permute-start(bf16[4,128,1024]{2,1,0:T(8,128)(2,1)} %get-tuple-element.48), channel_id=1, source_target_pairs={{0,4},{4,0},{8,12},{12,8},{16,20},{20,16},{24,28},{28,24},{1,5},{5... | collective-permute-start | bytes 3145736 | tf_op jit(solution)/shard_map/ppermute | solution.py:573
  171.2 22.3 %collective-permute-start.30 = (bf16[2,128,1024]{2,1,0:T(8,128)(2,1)S(1)}, bf16[2,128,1024]{2,1,0:T(8,128)(2,1)S(1)}, u32[]{:S(2)}, u32[]{:S(2)}) collective-permute-start(bf16[2,128,1024]{2,1,0:T(8,128)(2,1)S(1)} %collective-permute-done.28.refs_0_.refs_28_), channel_id=1, source_target_pairs={{0,4},{4,0},{8,12},{12,8},{16,20},{20,16},{24,28},{28,24},{1,5},{5... | collective-permute-start | bytes 1572872 | tf_op jit(solution)/shard_map/ppermute | solution.py:573
  171.6 22.3 %collective-permute-start.31 = (bf16[2,128,1024]{2,1,0:T(8,128)(2,1)S(1)}, bf16[2,128,1024]{2,1,0:T(8,128)(2,1)S(1)}, u32[]{:S(2)}, u32[]{:S(2)}) collective-permute-start(bf16[2,128,1024]{2,1,0:T(8,128)(2,1)S(1)} %collective-permute-done.29.refs_1_.refs_29_), channel_id=1, source_target_pairs={{0,4},{4,0},{8,12},{12,8},{16,20},{20,16},{24,28},{28,24},{1,5},{5... | collective-permute-start | bytes 1572872 | tf_op jit(solution)/shard_map/ppermute | solution.py:573
  193.5 72.1 %collective-permute-start.21 = (bf16[4,128,1024]{2,1,0:T(8,128)(2,1)}, bf16[4,128,1024]{2,1,0:T(8,128)(2,1)}, u32[]{:S(2)}, u32[]{:S(2)}) collective-permute-start(bf16[4,128,1024]{2,1,0:T(8,128)(2,1)} %get-tuple-element.46), channel_id=1, source_target_pairs={{0,4},{4,0},{8,12},{12,8},{16,20},{20,16},{24,28},{28,24},{1,5},{5... | collective-permute-start | bytes 3145736 | tf_op jit(solution)/shard_map/ppermute | solution.py:573
  216.6 24.9 %collective-permute-start.32 = (bf16[4,128,1024]{2,1,0:T(8,128)(2,1)}, bf16[4,128,1024]{2,1,0:T(8,128)(2,1)}, u32[]{:S(2)}, u32[]{:S(2)}) collective-permute-start(bf16[4,128,1024]{2,1,0:T(8,128)(2,1)} %get-tuple-element.50), channel_id=1, source_target_pairs={{0,4},{4,0},{8,12},{12,8},{16,20},{20,16},{24,28},{28,24},{1,5},{5... | collective-permute-start | bytes 3145736 | tf_op jit(solution)/shard_map/ppermute | solution.py:573
  241.3 3.4 %collective-permute-start.38 = (f32[8,48,128]{2,1,0:T(8,128)S(1)}, f32[8,48,128]{2,1,0:T(8,128)S(1)}, u32[]{:S(2)}, u32[]{:S(2)}) collective-permute-start(f32[8,48,128]{2,1,0:T(8,128)S(1)} %bitcast.132), channel_id=1, source_target_pairs={{0,4},{4,0},{8,12},{12,8},{16,20},{20,16},{24,28},{28,24},{1,5},{5... | collective-permute-start | bytes 589832 | tf_op jit(solution)/shard_map/ppermute | solution.py:573
  243.2 20.0 %collective-permute-start.33 = (bf16[2,128,1024]{2,1,0:T(8,128)(2,1)S(1)}, bf16[2,128,1024]{2,1,0:T(8,128)(2,1)S(1)}, u32[]{:S(2)}, u32[]{:S(2)}) collective-permute-start(bf16[2,128,1024]{2,1,0:T(8,128)(2,1)S(1)} %get-tuple-element.65), channel_id=1, source_target_pairs={{0,8},{4,12},{8,0},{12,4},{16,24},{20,28},{24,16},{28,20},{1,9},{5... | collective-permute-start | bytes 1572872 | tf_op jit(solution)/shard_map/ppermute | solution.py:573
  244.7 16.9 %collective-permute-start.39 = (f32[8,48,128]{2,1,0:T(8,128)S(1)}, f32[8,48,128]{2,1,0:T(8,128)S(1)}, u32[]{:S(2)}, u32[]{:S(2)}) collective-permute-start(f32[8,48,128]{2,1,0:T(8,128)S(1)} %bitcast.115), channel_id=1, source_target_pairs={{0,8},{4,12},{8,0},{12,4},{16,24},{20,28},{24,16},{28,20},{1,9},{5... | collective-permute-start | bytes 589832 | tf_op jit(solution)/shard_map/ppermute | solution.py:573
  245.4 20.2 %collective-permute-start.35 = (bf16[2,128,1024]{2,1,0:T(8,128)(2,1)S(1)}, bf16[2,128,1024]{2,1,0:T(8,128)(2,1)S(1)}, u32[]{:S(2)}, u32[]{:S(2)}) collective-permute-start(bf16[2,128,1024]{2,1,0:T(8,128)(2,1)S(1)} %get-tuple-element.66), channel_id=1, source_target_pairs={{0,16},{4,20},{8,24},{12,28},{16,0},{20,4},{24,8},{28,12},{1,17},{... | collective-permute-start | bytes 1572872 | tf_op jit(solution)/shard_map/ppermute | solution.py:573
  261.7 10.5 %collective-permute-start.40 = (f32[8,48,128]{2,1,0:T(8,128)S(1)}, f32[8,48,128]{2,1,0:T(8,128)}, u32[]{:S(2)}, u32[]{:S(2)}) collective-permute-start(f32[8,48,128]{2,1,0:T(8,128)S(1)} %bitcast.113), channel_id=1, source_target_pairs={{0,16},{4,20},{8,24},{12,28},{16,0},{20,4},{24,8},{28,12},{1,17},{... | collective-permute-start | bytes 589832 | tf_op jit(solution)/shard_map/ppermute | solution.py:573
  264.9 15.7 %collective-permute-start.37 = (bf16[2,128,1024]{2,1,0:T(8,128)(2,1)S(1)}, bf16[2,128,1024]{2,1,0:T(8,128)(2,1)}, u32[]{:S(2)}, u32[]{:S(2)}) collective-permute-start(bf16[2,128,1024]{2,1,0:T(8,128)(2,1)S(1)} %get-tuple-element.64), channel_id=1, source_target_pairs={{0,16},{4,20},{8,24},{12,28},{16,0},{20,4},{24,8},{28,12},{1,17},{... | collective-permute-start | bytes 1572872 | tf_op jit(solution)/shard_map/ppermute | solution.py:573
  267.3 15.0 %collective-permute-start.36 = (bf16[2,128,1024]{2,1,0:T(8,128)(2,1)S(1)}, bf16[2,128,1024]{2,1,0:T(8,128)(2,1)}, u32[]{:S(2)}, u32[]{:S(2)}) collective-permute-start(bf16[2,128,1024]{2,1,0:T(8,128)(2,1)S(1)} %get-tuple-element.62), channel_id=1, source_target_pairs={{0,8},{4,12},{8,0},{12,4},{16,24},{20,28},{24,16},{28,20},{1,9},{5... | collective-permute-start | bytes 1572872 | tf_op jit(solution)/shard_map/ppermute | solution.py:573
  268.8 22.8 %collective-permute-start.16 = (bf16[4,128,1024]{2,1,0:T(8,128)(2,1)}, bf16[4,128,1024]{2,1,0:T(8,128)(2,1)S(1)}, u32[]{:S(2)}, u32[]{:S(2)}) collective-permute-start(bf16[4,128,1024]{2,1,0:T(8,128)(2,1)} %get-tuple-element.44), channel_id=1, source_target_pairs={{0,4},{4,0},{8,12},{12,8},{16,20},{20,16},{24,28},{28,24},{1,5},{5... | collective-permute-start | bytes 3145736 | tf_op jit(solution)/shard_map/ppermute | solution.py:573
  271.5 19.0 %collective-permute-start.34 = (bf16[2,128,1024]{2,1,0:T(8,128)(2,1)S(1)}, bf16[2,128,1024]{2,1,0:T(8,128)(2,1)S(1)}, u32[]{:S(2)}, u32[]{:S(2)}) collective-permute-start(bf16[2,128,1024]{2,1,0:T(8,128)(2,1)S(1)} %get-tuple-element.63), channel_id=1, source_target_pairs={{0,16},{4,20},{8,24},{12,28},{16,0},{20,4},{24,8},{28,12},{1,17},{... | collective-permute-start | bytes 1572872 | tf_op jit(solution)/shard_map/ppermute | solution.py:573
  272.1 19.2 %collective-permute-start.22 = (bf16[2,128,1024]{2,1,0:T(8,128)(2,1)S(1)}, bf16[2,128,1024]{2,1,0:T(8,128)(2,1)S(1)}, u32[]{:S(2)}, u32[]{:S(2)}) collective-permute-start(bf16[2,128,1024]{2,1,0:T(8,128)(2,1)S(1)} %get-tuple-element.61), channel_id=1, source_target_pairs={{0,8},{4,12},{8,0},{12,4},{16,24},{20,28},{24,16},{28,20},{1,9},{5... | collective-permute-start | bytes 1572872 | tf_op jit(solution)/shard_map/ppermute | solution.py:573
  (36 other events, 765.3 us)
Sparse Core Ops, SparseCore 0:
  9.6 30.6 all-gather.8
  41.8 27.4 all-gather.6
  293.4 26.0 reduce-scatter.1

commit v2 on v0

--- a/solution.py
+++ b/solution.py
@@ -1,6 +1,8 @@
 import jax
 import jax.numpy as jnp
 from jax import lax
+from jax.experimental import pallas as pl
+from jax.experimental.pallas import tpu as pltpu
 from jax.sharding import PartitionSpec as P
 
 ADAPTER_SCALE = 2.0
@@ -88,7 +90,7 @@
     return (gradient_rows_out, shared_slice, owned_slice)
 
 
-def local(
+def general_local(
     tokens,
     output_gradient,
     routing,
@@ -197,9 +199,609 @@
     )
 
 
+LANES = 128
+TILE = 512
+SHARDS = 8
+VMEM_BYTES = 58 * 1024 * 1024
+HBM = pl.BlockSpec(memory_space=pl.ANY)
+VMEM = pl.BlockSpec(memory_space=pltpu.VMEM)
+SMEM = pl.BlockSpec(memory_space=pltpu.SMEM)
+
+
+def dot_nt(left, right):
+    return contract_pair(left, right, 1, 1)
+
+
+def dot_nn(left, right):
+    return contract_pair(left, right, 1, 0)
+
+
+def wide(value):
+    return value.astype(jnp.float32)
+
+
+def row_copies(pieces, per_block, target, sems):
+    deep, tokens_each, _ = pieces[0].shape
+    copies = []
+    for i, piece in enumerate(pieces):
+        block, part = divmod(i, per_block)
+        for k in range(deep):
+            slab = part * deep + k
+            copies.append(
+                pltpu.make_async_copy(
+                    piece.at[k],
+                    target.at[slab, pl.ds(block * tokens_each, tokens_each)],
+                    sems.at[i, k],
+                )
+            )
+    return copies
+
+
+def slab_lanes(slab_ref, slab, feat):
+    return pl.ds(pl.multiple_of(slab_ref[slab] * feat, feat), feat)
+
+
+def forward_kernel(n_pieces, per_block, *refs):
+    pieces = refs[:n_pieces]
+    (
+        slab_ref,
+        gate_hbm,
+        up_hbm,
+        lower_hbm,
+        gate_upper_ref,
+        up_upper_ref,
+        silu_out,
+        slope_out,
+        hidden_out,
+        low_out,
+    ) = refs[n_pieces : n_pieces + 10]
+    x_rows, weights, pre, saved, x_sems, w_sems, out_sems = refs[n_pieces + 10 :]
+    slabs, _, feat = x_rows.shape
+    hidden_here = gate_hbm.shape[0]
+    pair, rank = lower_hbm.shape[1], gate_upper_ref.shape[1]
+    x_copies = row_copies(pieces, per_block, x_rows, x_sems)
+    deep = pieces[0].shape[0]
+
+    def x_slab(slab):
+        part, k = divmod(slab, deep)
+        return [x_copies[(block * per_block + part) * deep + k] for block in range(SHARDS)]
+
+    def weight_copies(slab):
+        lanes = slab_lanes(slab_ref, slab, feat)
+        sides = (
+            (gate_hbm.at[:, lanes], 0, hidden_here),
+            (up_hbm.at[:, lanes], hidden_here, hidden_here),
+            (lower_hbm.at[slab], 2 * hidden_here, pair),
+        )
+        return [
+            pltpu.make_async_copy(
+                source, weights.at[slab, pl.ds(start, size)], w_sems.at[slab, i]
+            )
+            for i, (source, start, size) in enumerate(sides)
+        ]
+
+    for slab in range(slabs):
+        for copy in x_slab(slab) + weight_copies(slab):
+            copy.start()
+    for slab in range(slabs):
+        for copy in x_slab(slab) + weight_copies(slab):
+            copy.wait()
+        if slab == 0:
+            pre[...] = dot_nt(weights[0], x_rows[0])
+        else:
+            pre[...] += dot_nt(weights[slab], x_rows[slab])
+    low_out[...] = pre[2 * hidden_here :, :].astype(jnp.bfloat16)
+
+    def out_copies(tile):
+        at = pl.ds(pl.multiple_of(tile * LANES, LANES), LANES)
+        return [
+            pltpu.make_async_copy(saved.at[i, at], out.at[at], out_sems.at[i, tile])
+            for i, out in enumerate((silu_out, slope_out, hidden_out))
+        ]
+
+    tiles = hidden_here // LANES
+
+    @pl.loop(0, tiles)
+    def _(tile):
+        start = pl.multiple_of(tile * LANES, LANES)
+        at = pl.ds(start, LANES)
+        up_at = pl.ds(pl.multiple_of(hidden_here + start, LANES), LANES)
+        pre_gate = pre[at, :] + ADAPTER_SCALE * dot_nn(gate_upper_ref[at, :], low_out[:rank, :])
+        pre_up = pre[up_at, :] + ADAPTER_SCALE * dot_nn(up_upper_ref[at, :], low_out[rank:, :])
+        sigma = 1.0 / (1.0 + jnp.exp(-pre_gate))
+        silu = pre_gate * sigma
+        saved[0, at, :] = silu.astype(jnp.bfloat16)
+        saved[1, at, :] = (pre_up * (sigma * (1.0 + pre_gate * (1.0 - sigma)))).astype(
+            jnp.bfloat16
+        )
+        saved[2, at, :] = (silu * pre_up).astype(jnp.bfloat16)
+        for copy in out_copies(tile):
+            copy.start()
+
+    @pl.loop(0, tiles)
+    def _(tile):
+        for copy in out_copies(tile):
+            copy.wait()
+
+
+def forward_rows(pieces, per_block, slab_order, weights, lower_slabs, gate_upper, up_upper):
+    hidden_here, width = weights[0].shape
+    deep, tokens_each, feat = pieces[0].shape
+    rows = len(pieces) // per_block * tokens_each
+    slabs, pair, _ = lower_slabs.shape
+    kept = jax.ShapeDtypeStruct((hidden_here, rows), jnp.bfloat16)
+    return pl.pallas_call(
+        lambda *refs: forward_kernel(len(pieces), per_block, *refs),
+        out_shape=(kept, kept, kept, jax.ShapeDtypeStruct((pair, rows), jnp.bfloat16)),
+        in_specs=[HBM] * len(pieces) + [SMEM] + [HBM] * 3 + [VMEM] * 2,
+        out_specs=(HBM, HBM, HBM, VMEM),
+        scratch_shapes=[
+            pltpu.VMEM((slabs, rows, feat), jnp.bfloat16),
+            pltpu.VMEM((slabs, 2 * hidden_here + pair, feat), jnp.bfloat16),
+            pltpu.VMEM((2 * hidden_here + pair, rows), jnp.float32),
+            pltpu.VMEM((3, hidden_here, rows), jnp.bfloat16),
+            pltpu.SemaphoreType.DMA((len(pieces), deep)),
+            pltpu.SemaphoreType.DMA((slabs, 3)),
+            pltpu.SemaphoreType.DMA((3, hidden_here // LANES)),
+        ],
+        compiler_params=pltpu.CompilerParams(vmem_limit_bytes=VMEM_BYTES),
+        cost_estimate=pl.CostEstimate(
+            flops=8 * rows * hidden_here * width,
+            bytes_accessed=4 * hidden_here * width + 2 * rows * width,
+            transcendentals=rows * hidden_here,
+        ),
+        name="forward_rows",
+    )(*pieces, slab_order, *weights[:2], lower_slabs, gate_upper, up_upper)
+
+
+def backward_kernel(n_pieces, per_block, columns, *refs):
+    pieces = refs[:n_pieces]
+    blocks = n_pieces // per_block
+    (
+        slab_ref,
+        route_ref,
+        gate_hbm,
+        up_hbm,
+        down_hbm,
+        down_upper_hbm,
+        lower_hbm,
+        down_lower_ref,
+        down_lower_t_ref,
+        gate_upper_t_ref,
+        up_upper_t_ref,
+        silu_hbm,
+        slope_hbm,
+        hidden_hbm,
+        low_hbm,
+    ) = refs[n_pieces : n_pieces + 15]
+    terms_out = refs[n_pieces + 15 : n_pieces + 15 + blocks]
+    parts_out, owned_out, owned_down_out = refs[n_pieces + 15 + blocks : n_pieces + 18 + blocks]
+    (
+        g_rows,
+        down_w,
+        pair_w,
+        d_down,
+        d_cols,
+        d_pair,
+        silu,
+        slope,
+        hidden,
+        low,
+        in_sems,
+        d_sems,
+        p_sems,
+        f_sems,
+    ) = refs[n_pieces + 18 + blocks :]
+    slabs, rows, feat = g_rows.shape
+    tokens_each = rows // blocks
+    hidden_here = silu.shape[0]
+    rank, pair = down_lower_ref.shape[0], lower_hbm.shape[1]
+    deep = pieces[0].shape[0]
+    copies = row_copies(pieces, per_block, g_rows, in_sems)
+    run = rows // len(columns)
+    saved_copies = [
+        pltpu.make_async_copy(
+            source.at[:, pl.ds(column, run)], target.at[:, pl.ds(k * run, run)], f_sems.at[i, k]
+        )
+        for i, (source, target) in enumerate(
+            ((silu_hbm, silu), (slope_hbm, slope), (hidden_hbm, hidden), (low_hbm, low))
+        )
+        for k, column in enumerate(columns)
+    ]
+
+    def row_slab(slab):
+        part, k = divmod(slab, deep)
+        return [copies[(block * per_block + part) * deep + k] for block in range(blocks)]
+
+    def down_copies(slab):
+        return [
+            pltpu.make_async_copy(
+                down_hbm.at[:, slab_lanes(slab_ref, slab, feat)],
+                down_w.at[slab, pl.ds(0, hidden_here)],
+                d_sems.at[slab, 0],
+            ),
+            pltpu.make_async_copy(
+                down_upper_hbm.at[slab], down_w.at[slab, pl.ds(hidden_here, rank)], d_sems.at[slab, 1]
+            ),
+        ]
+
+    def pair_copies(slab):
+        lanes = slab_lanes(slab_ref, slab, feat)
+        sides = (
+            (gate_hbm.at[:, lanes], 0, hidden_here),
+            (up_hbm.at[:, lanes], hidden_here, hidden_here),
+            (lower_hbm.at[slab], 2 * hidden_here, pair),
+        )
+        return [
+            pltpu.make_async_copy(source, pair_w.at[slab, pl.ds(start, size)], p_sems.at[slab, i])
+            for i, (source, start, size) in enumerate(sides)
+        ]
+
+    for slab in range(slabs):
+        for copy in row_slab(slab) + down_copies(slab):
+            copy.start()
+    for copy in saved_copies:
+        copy.start()
+    for slab in range(slabs):
+        for copy in pair_copies(slab):
+            copy.start()
+    for slab in range(slabs):
+        for copy in row_slab(slab):
+            copy.wait()
+        g_rows[slab] = (route_ref[...] * g_rows[slab].astype(jnp.float32)).astype(jnp.bfloat16)
+        for copy in down_copies(slab):
+            copy.wait()
+        if slab == 0:
+            d_down[...] = dot_nt(down_w[0], g_rows[0])
+        else:
+            d_down[...] += dot_nt(down_w[slab], g_rows[slab])
+
+    low_down = d_down[hidden_here:, :].astype(jnp.bfloat16)
+    for copy in saved_copies:
+        copy.wait()
+
+    @pl.loop(0, hidden_here // LANES)
+    def _(tile):
+        start = pl.multiple_of(tile * LANES, LANES)
+        at = pl.ds(start, LANES)
+        up_at = pl.ds(pl.multiple_of(hidden_here + start, LANES), LANES)
+        d_hidden = d_down[at, :] + ADAPTER_SCALE * dot_nn(down_lower_t_ref[at, :], low_down)
+        d_gate = (d_hidden * wide(slope[at, :])).astype(jnp.bfloat16)
+        d_up = (d_hidden * wide(silu[at, :])).astype(jnp.bfloat16)
+        d_cols[at, :] = d_gate
+        d_cols[up_at, :] = d_up
+        d_pair[:, at] = d_gate.T
+        d_pair[:, up_at] = d_up.T
+
+    d_gate, d_up = d_cols[:hidden_here, :], d_cols[hidden_here:, :]
+    parts_out[0:rank, :] = dot_nn(gate_upper_t_ref[...], d_gate)
+    parts_out[rank : 2 * rank, :] = dot_nn(up_upper_t_ref[...], d_up)
+    parts_out[2 * rank :, :] = dot_nn(down_lower_ref[...], hidden[...])
+    d_pair[:, 2 * hidden_here :] = ADAPTER_SCALE * parts_out[:pair, :].astype(jnp.bfloat16).T
+
+    @pl.loop(0, slabs)
+    def _(slab):
+        for copy in pair_copies(slab):
+            copy.wait()
+
+        @pl.loop(0, feat // TILE)
+        def _(n):
+            lanes = pl.ds(pl.multiple_of(n * TILE, TILE), TILE)
+            term = dot_nn(d_pair[...], pair_w[slab, :, lanes]).astype(jnp.bfloat16)
+            for block, out in enumerate(terms_out):
+                out[slab, :, lanes] = term[block * tokens_each : (block + 1) * tokens_each]
+
+    owned_out[0] = ADAPTER_SCALE * dot_nt(low[:rank, :], d_gate)
+    owned_out[1] = ADAPTER_SCALE * dot_nt(low[rank:, :], d_up)
+    owned_down_out[...] = ADAPTER_SCALE * dot_nt(low_down, hidden[...])
+
+
+def backward_rows(
+    pieces,
+    per_block,
+    columns,
+    slab_order,
+    route_rows,
+    weights,
+    down_upper,
+    lower_slabs,
+    factors,
+    saved,
+):
+    hidden_here, width = weights[0].shape
+    slabs, rank, feat = down_upper.shape
+    pair = lower_slabs.shape[1]
+    deep, tokens_each, _ = pieces[0].shape
+    blocks = len(pieces) // per_block
+    rows = blocks * tokens_each
+    term = jax.ShapeDtypeStruct((slabs, tokens_each, feat), jnp.bfloat16)
+    results = pl.pallas_call(
+        lambda *refs: backward_kernel(len(pieces), per_block, columns, *refs),
+        out_shape=(term,) * blocks
+        + (
+            jax.ShapeDtypeStruct((3 * rank, rows), jnp.float32),
+            jax.ShapeDtypeStruct((2, rank, hidden_here), jnp.float32),
+            jax.ShapeDtypeStruct((rank, hidden_here), jnp.float32),
+        ),
+        in_specs=[HBM] * len(pieces) + [SMEM, VMEM] + [HBM] * 5 + [VMEM] * 4 + [HBM] * 4,
+        out_specs=(VMEM,) * (blocks + 3),
+        scratch_shapes=[
+            pltpu.VMEM((slabs, rows, feat), jnp.bfloat16),
+            pltpu.VMEM((slabs, hidden_here + rank, feat), jnp.bfloat16),
+            pltpu.VMEM((slabs, 2 * hidden_here + pair, feat), jnp.bfloat16),
+            pltpu.VMEM((hidden_here + rank, rows), jnp.float32),
+            pltpu.VMEM((2 * hidden_here, rows), jnp.bfloat16),
+            pltpu.VMEM((rows, 2 * hidden_here + pair), jnp.bfloat16),
+            pltpu.VMEM((hidden_here, rows), jnp.bfloat16),
+            pltpu.VMEM((hidden_here, rows), jnp.bfloat16),
+            pltpu.VMEM((hidden_here, rows), jnp.bfloat16),
+            pltpu.VMEM((2 * rank, rows), jnp.bfloat16),
+            pltpu.SemaphoreType.DMA((len(pieces), deep)),
+            pltpu.SemaphoreType.DMA((slabs, 2)),
+            pltpu.SemaphoreType.DMA((slabs, 3)),
+            pltpu.SemaphoreType.DMA((4, len(columns))),
+        ],
+        compiler_params=pltpu.CompilerParams(vmem_limit_bytes=VMEM_BYTES),
+        cost_estimate=pl.CostEstimate(
+            flops=12 * rows * hidden_here * width,
+            bytes_accessed=6 * hidden_here * width + 4 * rows * width,
+            transcendentals=0,
+        ),
+        name="backward_rows",
+    )(*pieces, slab_order, route_rows, *weights, down_upper, lower_slabs, *factors, *saved)
+    return results[:blocks], *results[blocks:]
+
+
+def shared_kernel(n_pieces, per_block, *refs):
+    x_pieces, dy_pieces = refs[:n_pieces], refs[n_pieces : 2 * n_pieces]
+    order_ref, slab_ref, sums_ref, down_sums_ref, pair_out, down_out = refs[
+        2 * n_pieces : 2 * n_pieces + 6
+    ]
+    x_rows, dy_rows, sums, down_sums, sems = refs[2 * n_pieces + 6 :]
+    deep, tokens_each, feat = x_pieces[0].shape
+    slabs = x_rows.shape[0]
+    copies = []
+    for side, (pieces, target) in enumerate(((x_pieces, x_rows), (dy_pieces, dy_rows))):
+        for i, piece in enumerate(pieces):
+            block, part = divmod(i, per_block)
+            start = pl.multiple_of(order_ref[block] * tokens_each, tokens_each)
+            for k in range(deep):
+                copies.append(
+                    pltpu.make_async_copy(
+                        piece.at[k],
+                        target.at[part * deep + k, pl.ds(start, tokens_each)],
+                        sems.at[side, i, k],
+                    )
+                )
+    for copy in copies:
+        copy.start()
+    for block in range(SHARDS):
+        lanes = pl.ds(pl.multiple_of(order_ref[block] * tokens_each, tokens_each), tokens_each)
+        sums[:, lanes] = sums_ref[block]
+        down_sums[:, lanes] = down_sums_ref[block]
+    for copy in copies:
+        copy.wait()
+
+    @pl.loop(0, slabs)
+    def _(slab):
+        @pl.loop(0, feat // TILE)
+        def _(n):
+            lanes = pl.ds(pl.multiple_of(n * TILE, TILE), TILE)
+            out = pl.ds(pl.multiple_of(slab_ref[slab] * feat + n * TILE, TILE), TILE)
+            pair_out[:, out] = ADAPTER_SCALE * dot_nn(
+                sums[...].astype(jnp.bfloat16), x_rows[slab, :, lanes]
+            )
+            down_out[:, out] = ADAPTER_SCALE * dot_nn(
+                down_sums[...].astype(jnp.bfloat16), dy_rows[slab, :, lanes]
+            )
+
+
+def shared_gradients(x_pieces, dy_pieces, per_block, order, slab_order, sums, down_sums):
+    deep, tokens_each, feat = x_pieces[0].shape
+    n_pieces = len(x_pieces)
+    slabs = deep * per_block
+    rows = SHARDS * tokens_each
+    pair, rank = sums.shape[1], down_sums.shape[1]
+    return pl.pallas_call(
+        lambda *refs: shared_kernel(n_pieces, per_block, *refs),
+        out_shape=(
+            jax.ShapeDtypeStruct((pair, slabs * feat), jnp.float32),
+            jax.ShapeDtypeStruct((rank, slabs * feat), jnp.float32),
+        ),
+        in_specs=[HBM] * (2 * n_pieces) + [SMEM, SMEM, VMEM, VMEM],
+        out_specs=(VMEM, VMEM),
+        scratch_shapes=[
+            pltpu.VMEM((slabs, rows, feat), jnp.bfloat16),
+            pltpu.VMEM((slabs, rows, feat), jnp.bfloat16),
+            pltpu.VMEM((pair, rows), jnp.float32),
+            pltpu.VMEM((rank, rows), jnp.float32),
+            pltpu.SemaphoreType.DMA((2, n_pieces, deep)),
+        ],
+        compiler_params=pltpu.CompilerParams(vmem_limit_bytes=VMEM_BYTES),
+        cost_estimate=pl.CostEstimate(
+            flops=16 * rows * pair * slabs * feat,
+            bytes_accessed=4 * rows * slabs * feat,
+            transcendentals=0,
+        ),
+        name="shared_gradients",
+    )(*x_pieces, *dy_pieces, order, slab_order, sums, down_sums)
+
+
+CORE, ACROSS, ALONG = 1, 2, 4
+
+
+def swap(value, bit, axis="dp"):
+    return lax.ppermute(value, axis, [(i, i ^ bit) for i in range(lax.axis_size(axis))])
+
+
+def slabs_of(block):
+    slabs = [block] + [swap(block, r, "expert") for r in range(1, lax.axis_size("expert"))]
+    half = len(slabs) // 2
+    return jnp.stack(slabs[:half]), jnp.stack(slabs[half:])
+
+
+def spread(lo, hi):
+    along_lo, across_hi = swap(lo, ALONG), swap(hi, ACROSS)
+    across_lo, along_hi = swap(lo, ACROSS), swap(hi, ALONG)
+    far_lo, far_hi = swap(along_lo, ACROSS), swap(across_hi, ALONG)
+    near = [(lo, hi), (across_lo, across_hi), (along_lo, along_hi), (far_lo, far_hi)]
+    blocks = []
+    for pair in near:
+        blocks.append(pair)
+        blocks.append(tuple(swap(part, CORE) for part in pair))
+    return blocks
+
+
+def added(left, right):
+    return (wide(left) + wide(right)).astype(jnp.bfloat16)
+
+
+def local(
+    tokens,
+    output_gradient,
+    routing,
+    router_gate_values,
+    gate_weight,
+    up_weight,
+    down_weight,
+    adapter_lower_gate,
+    adapter_upper_gate,
+    adapter_lower_up,
+    adapter_upper_up,
+    adapter_lower_down,
+    adapter_upper_down,
+):
+    experts = lax.axis_size("expert")
+    me, expert = lax.axis_index("dp"), lax.axis_index("expert")
+    tokens_each, feat = tokens.shape
+    rank = adapter_lower_gate.shape[1]
+    order = jnp.bitwise_xor(jnp.arange(SHARDS, dtype=jnp.int32), me.astype(jnp.int32))
+    slab_order = jnp.bitwise_xor(jnp.arange(experts, dtype=jnp.int32), expert.astype(jnp.int32))
+
+    named = routing[:, :, None] == jnp.arange(experts, dtype=jnp.int32)[None, None, :]
+    weight_of = jnp.sum(jnp.where(named, router_gate_values[:, :, None], 0.0), axis=1)
+    all_routes = lax.all_gather(weight_of.T, "dp", axis=0, tiled=False)
+
+    def slabs_first(factor):
+        return factor.reshape(factor.shape[0], experts, feat).transpose(1, 0, 2)[slab_order]
+
+    lower_slabs = slabs_first(
+        jnp.concatenate([adapter_lower_gate[0], adapter_lower_up[0]], axis=0)
+    )
+    down_upper = slabs_first(adapter_upper_down[0].T)
+    down_lower = adapter_lower_down[0]
+    factors = (down_lower, down_lower.T, adapter_upper_gate[0].T, adapter_upper_up[0].T)
+
+    x_lo, x_hi = slabs_of(tokens)
+    x_blocks = spread(x_lo, x_hi)
+    (across_lo, across_hi) = x_blocks[2]
+    output_gradient, across_lo = lax.optimization_barrier((output_gradient, across_lo))
+    x_blocks[2] = (across_lo, across_hi)
+    dy_lo, dy_hi = slabs_of(output_gradient)
+    dy_lo, dy_hi, x_blocks[2], x_blocks[4] = lax.optimization_barrier(
+        (dy_lo, dy_hi, x_blocks[2], x_blocks[4])
+    )
+    dy_blocks = spread(dy_lo, dy_hi)
+    x_blocks[6], all_routes = lax.optimization_barrier((x_blocks[6], all_routes))
+    route = lax.dynamic_index_in_dim(all_routes, expert, axis=1, keepdims=False)[order]
+    route_column = route.reshape(SHARDS, tokens_each, 1)
+    x_pieces = [part for pair in x_blocks for part in pair]
+    dy_pieces = [part for pair in dy_blocks for part in pair]
+
+    weights = (gate_weight[0], up_weight[0], down_weight[0])
+    saved = forward_rows(
+        x_pieces,
+        2,
+        slab_order,
+        weights,
+        lower_slabs,
+        adapter_upper_gate[0],
+        adapter_upper_up[0],
+    )
+    terms, parts, owned, owned_down = {}, {}, [], []
+    for group in ((6, 7, 0, 1), (2, 3, 4, 5)):
+        columns = [j * tokens_each for j in group[::2]]
+        rows_out, part, own, own_down = backward_rows(
+            [piece for j in group for piece in dy_blocks[j]],
+            2,
+            columns,
+            slab_order,
+            jnp.concatenate([route_column[j] for j in group], axis=0),
+            weights,
+            down_upper,
+            lower_slabs,
+            factors,
+            saved,
+        )
+        for i, j in enumerate(group):
+            terms[j] = rows_out[i]
+            parts[j] = part[:, i * tokens_each : (i + 1) * tokens_each]
+        owned.append(own)
+        owned_down.append(own_down)
+
+    half = experts // 2
+    lo, hi = slice(0, half), slice(half, experts)
+    far_a, far_b = terms[6], swap(terms[7], CORE)
+    own_a, own_b = terms[0], swap(terms[1], CORE)
+    far_lo = swap(added(far_a[lo], far_b[lo]), ACROSS)
+    far_hi = swap(added(far_a[hi], far_b[hi]), ALONG)
+    across_a, across_b = terms[2], swap(terms[3], CORE)
+    along_a, along_b = terms[4], swap(terms[5], CORE)
+    got_across_hi = swap(added(added(across_a[hi], across_b[hi]), far_hi), ACROSS)
+    got_along_hi = swap(added(along_a[hi], along_b[hi]), ALONG)
+    got_across_lo = swap(added(across_a[lo], across_b[lo]), ACROSS)
+    got_along_lo = swap(added(added(along_a[lo], along_b[lo]), far_lo), ALONG)
+    rows_hi = wide(own_a[hi]) + wide(own_b[hi]) + wide(got_across_hi) + wide(got_along_hi)
+    rows_lo = wide(own_a[lo]) + wide(own_b[lo]) + wide(got_across_lo) + wide(got_along_lo)
+    rows_hi, rows_lo = rows_hi.astype(jnp.bfloat16), rows_lo.astype(jnp.bfloat16)
+    grad_x = wide(rows_lo[0])
+    for r in range(1, experts):
+        piece = rows_lo[r] if r < half else rows_hi[r - half]
+        grad_x = grad_x + wide(swap(piece, r, "expert"))
+    grad_x = grad_x.astype(jnp.bfloat16)
+
+    total = jnp.stack([parts[j] for j in range(SHARDS)], axis=0)
+    for bit in (CORE, ACROSS, ALONG):
+        other = swap(total.reshape(SHARDS, 3 * rank, tokens_each), bit)
+        shape = (SHARDS // (2 * bit), 2, bit, 3 * rank, tokens_each)
+        total = total.reshape(shape) + other.reshape(shape)[:, ::-1]
+    total = total.reshape(SHARDS, 3 * rank, tokens_each)
+    grad_pair, grad_down = shared_gradients(
+        x_pieces,
+        dy_pieces,
+        2,
+        order,
+        slab_order,
+        total[:, : 2 * rank],
+        total[:, 2 * rank :] * route[:, None, :],
+    )
+    owned_sum = sum(owned[1:], owned[0])
+    return (
+        grad_x,
+        grad_pair[None, :rank],
+        owned_sum[0].T[None],
+        grad_pair[None, rank:],
+        owned_sum[1].T[None],
+        sum(owned_down[1:], owned_down[0])[None],
+        grad_down.T[None],
+    )
+
+
+def plan(tokens, *others):
+    experts, tokens_each, hidden_here = lax.axis_size("expert"), tokens.shape[0], others[3].shape[1]
+    planned = (
+        lax.axis_size("dp") == SHARDS
+        and experts in (2, 4)
+        and hidden_here % LANES == 0
+        and tokens_each % LANES == 0
+        and tokens.shape[1] % TILE == 0
+    )
+    return (local if planned else general_local)(tokens, *others)
+
+
 def solution(mesh):
     return jax.shard_map(
-        local,
+        plan,
         mesh=mesh,
         in_specs=(
             P("dp", "expert"),

time: 445 us -> 293 us (0.66); the launches traced: 436 us -> 292 us
  matrix products: 135 us -> 0 us
  Pallas kernels: 0 us -> 92 us
  waiting for transfers between devices: 188 us -> 112 us
  blocking collectives: 60 us -> 17.3 us
  starting transfers between devices: 4.72 us -> 37.4 us
  between operations: 14.5 us -> 1.12 us
  local copies, waits for them, and re-layouts: 24.8 us -> 20.2 us
    dot_general x20 -> x0, matrix products: 135 us -> none  [contract_pair(): lax.dot_general(left, right, (((left_axis,), (right_axis,)), ((), ())), p...]
    ppermute x0 -> x50, waiting for transfers between devices: none -> 112 us  [swap(): lax.ppermute(value, axis, [(i, i ^ bit) for i in range(lax.axis_size(axis...]
    pallas_call x0 -> x4, Pallas kernels: none -> 92 us  [the longest x2 53.8 us: backward_rows(): pl.pallas_call(lambda *refs: backward_kernel(len(pieces), per_block, colu...]
    all_gather x2 -> x0, waiting for transfers between devices: 74.4 us -> none  [the longest x1 50.1 us: local(): lax.all_gather(recv_x[0], 'dp', axis=0, tiled=True)]
    reduce_scatter x1 -> x0, waiting for transfers between devices: 64.2 us -> none  [local(): lax.psum_scatter(rows_part.astype(jnp.bfloat16), 'dp', scatter_dimension=...]
    all_to_all x2 -> x0, blocking collectives: 60 us -> none  [the longest x1 31.9 us: local(): lax.all_to_all(send_dy, 'expert', split_axis=0, concat_axis=2, tiled=True)]
    psum x1 -> x0, waiting for transfers between devices: 49.3 us -> none  [local(): lax.psum(shared_slice[0].astype(jnp.bfloat16), 'dp').astype(jnp.float32)]
    ppermute x0 -> x50, starting transfers between devices: none -> 37.4 us  [swap(): lax.ppermute(value, axis, [(i, i ^ bit) for i in range(lax.axis_size(axis...]
  transfers between devices with their start and end apart: 5 -> 50, of which waited for: 4 -> 15; matrix products, arithmetic and copies ran while one was open for 9% -> 10% of each run, Pallas kernels for 0% -> 31%
where the time goes in v2:
time: 293 us; the launch traced here: 292 us
  waiting for transfers between devices  112 us (38%)
  Pallas kernels  92 us (31%)
  starting transfers between devices  37.4 us (13%)
  local copies, waits for them, and re-layouts  20.2 us (7%)
  blocking collectives  17.3 us (6%)
  other arithmetic  12.9 us (4%)
    ppermute x50, waiting for transfers between devices, swap(): lax.ppermute(value, axis, [(i, i ^ bit) for i in range(lax.axis_size(axis...  112 us
    pallas_call x2, Pallas kernels, backward_rows(): pl.pallas_call(lambda *refs: backward_kernel(len(pieces), per_block, colu...  53.8 us
    ppermute x50, starting transfers between devices, swap(): lax.ppermute(value, axis, [(i, i ^ bit) for i in range(lax.axis_size(axis...  37.4 us
    pallas_call x1, Pallas kernels, forward_rows(): pl.pallas_call(lambda *refs: forward_kernel(len(pieces), per_block, *refs...  26.6 us
    all_gather x1, blocking collectives, local(): all_routes = lax.all_gather(weight_of.T, 'dp', axis=0, tiled=False)  17.3 us
    pallas_call x1, Pallas kernels, shared_gradients(): pl.pallas_call(lambda *refs: shared_kernel(n_pieces, per_block, *refs), o...  11.7 us
  transfers between devices with their start and end apart: 50, of which 15 were waited for; matrix products, arithmetic and copies ran while one was open for 10% of the time, Pallas kernels for 31%

profile of v2, /device:TPU:0, one launch (start us, length us, event | category | flops | bytes accessed | tf_op | source)
XLA Modules:
  0.0 292.4 jit_solution(9259260769007108809)
XLA Ops:
  0.7 3.1 %collective-permute-start = (bf16[128,1024]{1,0:T(8,128)(2,1)}, bf16[128,1024]{1,0:T(8,128)(2,1)S(1)}, u32[]{:S(2)}, u32[]{:S(2)}) collective-permute-start(bf16[128,1024]{1,0:T(8,128)(2,1)} %param.13), channel_id=1, source_target_pairs={{0,1},{1,0},{2,3},{3,2},{4,5},{5,4},{6,7},{7,6},{8,9},{9,8},{10,11... | collective-permute-start | bytes 786440 | tf_op jit(solution)/shard_map/ppermute | solution.py:634
  3.7 2.5 collective-permute-start.6
  6.3 4.4 %collective-permute-done = bf16[128,1024]{1,0:T(8,128)(2,1)S(1)} collective-permute-done((bf16[128,1024]{1,0:T(8,128)(2,1)}, bf16[128,1024]{1,0:T(8,128)(2,1)S(1)}, u32[]{:S(2)}, u32[]{:S(2)}) %collective-permute-start) | collective-permute-done | bytes 262176 | tf_op jit(solution)/shard_map/ppermute | solution.py:634
  10.8 1.0 pad_maximum_fusion.refs_0_
  11.8 1.6 collective-permute-start.1
  13.3 6.0 %collective-permute-done.6 = bf16[128,1024]{1,0:T(8,128)(2,1)S(1)} collective-permute-done((bf16[128,1024]{1,0:T(8,128)(2,1)}, bf16[128,1024]{1,0:T(8,128)(2,1)S(1)}, u32[]{:S(2)}, u32[]{:S(2)}) %collective-permute-start.6) | collective-permute-done | bytes 262176 | tf_op jit(solution)/shard_map/ppermute | solution.py:634
  19.3 10.1 %collective-permute-done.5 = bf16[128,1024]{1,0:T(8,128)(2,1)S(1)} collective-permute-done((bf16[128,1024]{1,0:T(8,128)(2,1)}, bf16[128,1024]{1,0:T(8,128)(2,1)S(1)}, u32[]{:S(2)}, u32[]{:S(2)}) %collective-permute-start.5) | collective-permute-done | bytes 262176 | tf_op jit(solution)/shard_map/ppermute | solution.py:634
  29.5 1.6 collective-permute-start.7
  31.1 1.5 collective-permute-start.8
  33.1 2.7 collective-permute-start.4
  35.8 6.6 %collective-permute-done.7.refs_5_ = bf16[2,128,1024]{2,1,0:T(8,128)(2,1)S(1)} collective-permute-done((bf16[2,128,1024]{2,1,0:T(8,128)(2,1)S(1)}, bf16[2,128,1024]{2,1,0:T(8,128)(2,1)S(1)}, u32[]{:S(2)}, u32[]{:S(2)}) %collective-permute-start.7) | collective-permute-done | bytes 524320 | tf_op jit(solution)/shard_map/ppermute | solution.py:634
  42.4 3.7 %collective-permute-done.8.refs_8_ = bf16[2,128,1024]{2,1,0:T(8,128)(2,1)} collective-permute-done((bf16[2,128,1024]{2,1,0:T(8,128)(2,1)S(1)}, bf16[2,128,1024]{2,1,0:T(8,128)(2,1)}, u32[]{:S(2)}, u32[]{:S(2)}) %collective-permute-start.8) | collective-permute-done | bytes 524320 | tf_op jit(solution)/shard_map/ppermute | solution.py:634
  46.0 8.8 %collective-permute-done.9.refs_9_ = bf16[2,128,1024]{2,1,0:T(8,128)(2,1)S(1)} collective-permute-done((bf16[2,128,1024]{2,1,0:T(8,128)(2,1)S(1)}, bf16[2,128,1024]{2,1,0:T(8,128)(2,1)S(1)}, u32[]{:S(2)}, u32[]{:S(2)}) %collective-permute-start.9) | collective-permute-done | bytes 524320 | tf_op jit(solution)/shard_map/ppermute | solution.py:634
  55.9 1.8 collective-permute-done.3
  57.7 1.5 collective-permute-start.19
  59.2 0.9 copy.93
  60.1 1.0 concatenate.16
  61.2 1.0 concatenate.15
  62.2 1.2 gather_fusion.1
  63.5 1.3 gather_fusion.2
  64.7 1.6 copy.83
  66.3 1.6 copy.84.refs_20_
  67.9 1.6 copy.85.refs_21_
  69.5 1.0 pad_maximum_fusion.1.refs_4_.refs_16_
  70.5 1.3 pad_maximum_fusion.2.refs_5_.refs_17_
  73.7 17.3 %all-gather.1 = f32[8,4,128]{2,1,0:T(4,128)S(1)} all-gather(f32[1,4,128]{2,1,0:T(4,128)S(1)} %bitcast.144), channel_id=2, replica_groups=mesh['dp'=8,'expert'=4] {'dp'}, dimensions={0}, use_global_device_ids=true | all-gather | bytes 18432 | tf_op jit(solution)/shard_map/all_gather | solution.py:683
  92.8 1.3 collective-permute-start.32
  97.7 9.2 %collective-permute-done.29.refs_0_.refs_20_ = bf16[2,128,1024]{2,1,0:T(8,128)(2,1)} collective-permute-done((bf16[2,128,1024]{2,1,0:T(8,128)(2,1)S(1)}, bf16[2,128,1024]{2,1,0:T(8,128)(2,1)}, u32[]{:S(2)}, u32[]{:S(2)}) %collective-permute-start.29) | collective-permute-done | bytes 524320 | tf_op jit(solution)/shard_map/ppermute | solution.py:634
  108.2 9.4 %collective-permute-done.11.refs_0_.refs_28_ = bf16[2,128,1024]{2,1,0:T(8,128)(2,1)} collective-permute-done((bf16[2,128,1024]{2,1,0:T(8,128)(2,1)}, bf16[2,128,1024]{2,1,0:T(8,128)(2,1)}, u32[]{:S(2)}, u32[]{:S(2)}) %collective-permute-start.11) | collective-permute-done | bytes 524320 | tf_op jit(solution)/shard_map/ppermute | solution.py:634
  117.6 26.6 %forward_rows.1 = (bf16[896,1024]{1,0:T(8,128)(2,1)}, bf16[896,1024]{1,0:T(8,128)(2,1)}, bf16[896,1024]{1,0:T(8,128)(2,1)}, bf16[32,1024]{1,0:T(8,128)(2,1)}) custom-call(bf16[2,128,1024]{2,1,0:T(8,128)(2,1)} %copy-done, bf16[2,128,1024]{2,1,0:T(8,128)(2,1)} %copy-done.1, bf16[2,128,1024]{2,1,0:T(8,128)(2,1)} %collective-permute-done.20.refs_2_, ...), custom_call_target="tpu_custom_call" | custom-call | flops 30064771072 | bytes 23068672 | tf_op jit(solution)/shard_map/forward_rows/pallas_call | solution.py:333
  146.4 26.9 %backward_rows.3 = (bf16[4,128,1024]{2,1,0:T(8,128)(2,1)}, bf16[4,128,1024]{2,1,0:T(8,128)(2,1)}, bf16[4,128,1024]{2,1,0:T(8,128)(2,1)}, bf16[4,128,1024]{2,1,0:...) custom-call(bf16[2,128,1024]{2,1,0:T(8,128)(2,1)} %collective-permute-done.29.refs_0_.refs_20_, ...), custom_call_target="tpu_custom_call" | custom-call | flops 22548578304 | bytes 30408704 | tf_op jit(solution)/shard_map/backward_rows/pallas_call | solution.py:518
  174.5 26.9 %backward_rows.2 = (bf16[4,128,1024]{2,1,0:T(8,128)(2,1)}, bf16[4,128,1024]{2,1,0:T(8,128)(2,1)}, bf16[4,128,1024]{2,1,0:T(8,128)(2,1)}, bf16[4,128,1024]{2,1,0:...) custom-call(bf16[2,128,1024]{2,1,0:T(8,128)(2,1)} %collective-permute-done.11.refs_0_.refs_28_, ...), custom_call_target="tpu_custom_call" | custom-call | flops 22548578304 | bytes 30408704 | tf_op jit(solution)/shard_map/backward_rows/pallas_call | solution.py:518
  206.7 1.6 add_convert_fusion.7
  209.1 1.4 collective-permute-start.48
  210.5 1.4 add_bitcast_fusion
  212.0 14.8 %collective-permute-done.48 = f32[8,48,128]{2,1,0:T(8,128)S(1)} collective-permute-done((f32[8,48,128]{2,1,0:T(8,128)S(1)}, f32[8,48,128]{2,1,0:T(8,128)S(1)}, u32[]{:S(2)}, u32[]{:S(2)}) %collective-permute-start.48) | collective-permute-done | bytes 196640 | tf_op jit(solution)/shard_map/ppermute | solution.py:634
  227.4 1.4 collective-permute-start.49
  230.1 11.5 %collective-permute-done.42 = bf16[2,128,1024]{2,1,0:T(8,128)(2,1)S(1)} collective-permute-done((bf16[2,128,1024]{2,1,0:T(8,128)(2,1)S(1)}, bf16[2,128,1024]{2,1,0:T(8,128)(2,1)S(1)}, u32[]{:S(2)}, u32[]{:S(2)}) %collective-permute-start.42) | collective-permute-done | bytes 524320 | tf_op jit(solution)/shard_map/ppermute | solution.py:634
  242.9 1.3 collective-permute-start.44
  244.2 1.7 collective-permute-done.49
  247.9 11.7 %shared_gradients.1 = (f32[32,4096]{1,0:T(8,128)}, f32[16,4096]{1,0:T(8,128)}) custom-call(bf16[2,128,1024]{2,1,0:T(8,128)(2,1)} %copy-done, bf16[2,128,1024]{2,1,0:T(8,128)(2,1)} %copy-done.1, bf16[2,128,1024]{2,1,0:T(8,128)(2,1)} %collective-permute-done.20.refs_2_, bf16[2,128,1024]{2,1,0:T(8,128)(2,1)} %collective-permute-done.21.refs_3_, ...), custom_call_target="tpu_custom_call" | custom-call | flops 2147483648 | bytes 16777216 | tf_op jit(solution)/shard_map/shared_gradients/pallas_call | solution.py:605
  259.6 7.2 %collective-permute-done.44 = bf16[2,128,1024]{2,1,0:T(8,128)(2,1)S(1)} collective-permute-done((bf16[2,128,1024]{2,1,0:T(8,128)(2,1)S(1)}, bf16[2,128,1024]{2,1,0:T(8,128)(2,1)S(1)}, u32[]{:S(2)}, u32[]{:S(2)}) %collective-permute-start.44) | collective-permute-done | bytes 524320 | tf_op jit(solution)/shard_map/ppermute | solution.py:634
  266.8 1.9 add_convert_fusion.5
  268.8 2.3 collective-permute-start.46
  271.1 2.2 collective-permute-start.41
  273.3 1.9 slice_bitcast_fusion.4
  275.2 4.8 %collective-permute-done.46 = bf16[128,1024]{1,0:T(8,128)(2,1)S(1)} collective-permute-done((bf16[128,1024]{1,0:T(8,128)(2,1)S(1)}, bf16[128,1024]{1,0:T(8,128)(2,1)S(1)}, u32[]{:S(2)}, u32[]{:S(2)}) %collective-permute-start.46) | collective-permute-done | bytes 262176 | tf_op jit(solution)/shard_map/ppermute | solution.py:634
  280.0 11.5 %collective-permute-done.45 = bf16[128,1024]{1,0:T(8,128)(2,1)S(1)} collective-permute-done((bf16[128,1024]{1,0:T(8,128)(2,1)S(1)}, bf16[128,1024]{1,0:T(8,128)(2,1)S(1)}, u32[]{:S(2)}, u32[]{:S(2)}) %collective-permute-start.45) | collective-permute-done | bytes 262176 | tf_op jit(solution)/shard_map/ppermute | solution.py:634
  (162 shorter events, 26.0 us)
Async XLA Ops:
  0.7 10.1 %collective-permute-start = (bf16[128,1024]{1,0:T(8,128)(2,1)}, bf16[128,1024]{1,0:T(8,128)(2,1)S(1)}, u32[]{:S(2)}, u32[]{:S(2)}) collective-permute-start(bf16[128,1024]{1,0:T(8,128)(2,1)} %param.13), channel_id=1, source_target_pairs={{0,1},{1,0},{2,3},{3,2},{4,5},{5,4},{6,7},{7,6},{8,9},{9,8},{10,11... | collective-permute-start | bytes 786440 | tf_op jit(solution)/shard_map/ppermute | solution.py:634
  3.7 15.6 %collective-permute-start.6 = (bf16[128,1024]{1,0:T(8,128)(2,1)}, bf16[128,1024]{1,0:T(8,128)(2,1)S(1)}, u32[]{:S(2)}, u32[]{:S(2)}) collective-permute-start(bf16[128,1024]{1,0:T(8,128)(2,1)} %param.13), channel_id=1, source_target_pairs={{0,3},{1,2},{2,1},{3,0},{4,7},{5,6},{6,5},{7,4},{8,11},{9,10},{10,... | collective-permute-start | bytes 786440 | tf_op jit(solution)/shard_map/ppermute | solution.py:634
  6.2 23.2 %collective-permute-start.5 = (bf16[128,1024]{1,0:T(8,128)(2,1)}, bf16[128,1024]{1,0:T(8,128)(2,1)S(1)}, u32[]{:S(2)}, u32[]{:S(2)}) collective-permute-start(bf16[128,1024]{1,0:T(8,128)(2,1)} %param.13), channel_id=1, source_target_pairs={{0,2},{1,3},{2,0},{3,1},{4,6},{5,7},{6,4},{7,5},{8,10},{9,11},{10,... | collective-permute-start | bytes 786440 | tf_op jit(solution)/shard_map/ppermute | solution.py:634
  11.8 21.3 %collective-permute-start.1 = (bf16[2,128,1024]{2,1,0:T(8,128)(2,1)S(1)}, bf16[2,128,1024]{2,1,0:T(8,128)(2,1)S(1)}, u32[]{:S(2)}, u32[]{:S(2)}) collective-permute-start(bf16[2,128,1024]{2,1,0:T(8,128)(2,1)S(1)} %pad_maximum_fusion.refs_0_), channel_id=1, source_target_pairs={{0,8},{4,12},{8,0},{12,4},{16,24},{20,28},{24,16},{28,20},{1,9},{5... | collective-permute-start | bytes 1572872 | tf_op jit(solution)/shard_map/ppermute | solution.py:634
  29.5 12.9 %collective-permute-start.7 = (bf16[2,128,1024]{2,1,0:T(8,128)(2,1)S(1)}, bf16[2,128,1024]{2,1,0:T(8,128)(2,1)S(1)}, u32[]{:S(2)}, u32[]{:S(2)}) collective-permute-start(bf16[2,128,1024]{2,1,0:T(8,128)(2,1)S(1)} %pad_maximum_fusion.3.refs_1_), channel_id=1, source_target_pairs={{0,8},{4,12},{8,0},{12,4},{16,24},{20,28},{24,16},{28,20},{1,9},{5... | collective-permute-start | bytes 1572872 | tf_op jit(solution)/shard_map/ppermute | solution.py:634
  31.1 15.0 %collective-permute-start.8 = (bf16[2,128,1024]{2,1,0:T(8,128)(2,1)S(1)}, bf16[2,128,1024]{2,1,0:T(8,128)(2,1)}, u32[]{:S(2)}, u32[]{:S(2)}) collective-permute-start(bf16[2,128,1024]{2,1,0:T(8,128)(2,1)S(1)} %pad_maximum_fusion.refs_0_), channel_id=1, source_target_pairs={{0,16},{4,20},{8,24},{12,28},{16,0},{20,4},{24,8},{28,12},{1,17},{... | collective-permute-start | bytes 1572872 | tf_op jit(solution)/shard_map/ppermute | solution.py:634
  32.6 22.2 %collective-permute-start.9 = (bf16[2,128,1024]{2,1,0:T(8,128)(2,1)S(1)}, bf16[2,128,1024]{2,1,0:T(8,128)(2,1)S(1)}, u32[]{:S(2)}, u32[]{:S(2)}) collective-permute-start(bf16[2,128,1024]{2,1,0:T(8,128)(2,1)S(1)} %pad_maximum_fusion.3.refs_1_), channel_id=1, source_target_pairs={{0,16},{4,20},{8,24},{12,28},{16,0},{20,4},{24,8},{28,12},{1,17},{... | collective-permute-start | bytes 1572872 | tf_op jit(solution)/shard_map/ppermute | solution.py:634
  33.1 21.7 %collective-permute-start.2 = (bf16[128,1024]{1,0:T(8,128)(2,1)}, bf16[128,1024]{1,0:T(8,128)(2,1)S(1)}, u32[]{:S(2)}, u32[]{:S(2)}) collective-permute-start(bf16[128,1024]{1,0:T(8,128)(2,1)} %param.14), channel_id=1, source_target_pairs={{0,1},{1,0},{2,3},{3,2},{4,5},{5,4},{6,7},{7,6},{8,9},{9,8},{10,11... | collective-permute-start | bytes 786440 | tf_op jit(solution)/shard_map/ppermute | solution.py:634
  33.1 22.2 %collective-permute-start.4 = (bf16[128,1024]{1,0:T(8,128)(2,1)}, bf16[128,1024]{1,0:T(8,128)(2,1)}, u32[]{:S(2)}, u32[]{:S(2)}) collective-permute-start(bf16[128,1024]{1,0:T(8,128)(2,1)} %param.14), channel_id=1, source_target_pairs={{0,3},{1,2},{2,1},{3,0},{4,7},{5,6},{6,5},{7,4},{8,11},{9,10},{10,... | collective-permute-start | bytes 786440 | tf_op jit(solution)/shard_map/ppermute | solution.py:634
  42.4 15.3 %collective-permute-start.3 = (bf16[128,1024]{1,0:T(8,128)(2,1)}, bf16[128,1024]{1,0:T(8,128)(2,1)S(1)}, u32[]{:S(2)}, u32[]{:S(2)}) collective-permute-start(bf16[128,1024]{1,0:T(8,128)(2,1)} %param.14), channel_id=1, source_target_pairs={{0,2},{1,3},{2,0},{3,1},{4,6},{5,7},{6,4},{7,5},{8,10},{9,11},{10,... | collective-permute-start | bytes 786440 | tf_op jit(solution)/shard_map/ppermute | solution.py:634
  46.0 25.7 %collective-permute-start.20 = (bf16[2,128,1024]{2,1,0:T(8,128)(2,1)S(1)}, bf16[2,128,1024]{2,1,0:T(8,128)(2,1)}, u32[]{:S(2)}, u32[]{:S(2)}) collective-permute-start(bf16[2,128,1024]{2,1,0:T(8,128)(2,1)S(1)} %pad_maximum_fusion.refs_0_), channel_id=1, source_target_pairs={{0,4},{4,0},{8,12},{12,8},{16,20},{20,16},{24,28},{28,24},{1,5},{5... | collective-permute-start | bytes 1572872 | tf_op jit(solution)/shard_map/ppermute | solution.py:634
  54.8 17.0 %collective-permute-start.21 = (bf16[2,128,1024]{2,1,0:T(8,128)(2,1)S(1)}, bf16[2,128,1024]{2,1,0:T(8,128)(2,1)}, u32[]{:S(2)}, u32[]{:S(2)}) collective-permute-start(bf16[2,128,1024]{2,1,0:T(8,128)(2,1)S(1)} %pad_maximum_fusion.3.refs_1_), channel_id=1, source_target_pairs={{0,4},{4,0},{8,12},{12,8},{16,20},{20,16},{24,28},{28,24},{1,5},{5... | collective-permute-start | bytes 1572872 | tf_op jit(solution)/shard_map/ppermute | solution.py:634
  54.8 18.3 %collective-permute-start.22 = (bf16[2,128,1024]{2,1,0:T(8,128)(2,1)S(1)}, bf16[2,128,1024]{2,1,0:T(8,128)(2,1)}, u32[]{:S(2)}, u32[]{:S(2)}) collective-permute-start(bf16[2,128,1024]{2,1,0:T(8,128)(2,1)S(1)} %collective-permute-done.1.refs_4_), channel_id=1, source_target_pairs={{0,4},{4,0},{8,12},{12,8},{16,20},{20,16},{24,28},{28,24},{1,5},{5... | collective-permute-start | bytes 1572872 | tf_op jit(solution)/shard_map/ppermute | solution.py:634
  55.3 17.0 %collective-permute-start.18 = (bf16[2,128,1024]{2,1,0:T(8,128)(2,1)}, bf16[2,128,1024]{2,1,0:T(8,128)(2,1)}, u32[]{:S(2)}, u32[]{:S(2)}) collective-permute-start(bf16[2,128,1024]{2,1,0:T(8,128)(2,1)} %collective-permute-done.8.refs_8_), channel_id=1, source_target_pairs={{0,8},{4,12},{8,0},{12,4},{16,24},{20,28},{24,16},{28,20},{1,9},{5... | collective-permute-start | bytes 1572872 | tf_op jit(solution)/shard_map/ppermute | solution.py:634
  57.7 14.8 %collective-permute-start.19 = (bf16[2,128,1024]{2,1,0:T(8,128)(2,1)S(1)}, bf16[2,128,1024]{2,1,0:T(8,128)(2,1)}, u32[]{:S(2)}, u32[]{:S(2)}) collective-permute-start(bf16[2,128,1024]{2,1,0:T(8,128)(2,1)S(1)} %collective-permute-done.7.refs_5_), channel_id=1, source_target_pairs={{0,16},{4,20},{8,24},{12,28},{16,0},{20,4},{24,8},{28,12},{1,17},{... | collective-permute-start | bytes 1572872 | tf_op jit(solution)/shard_map/ppermute | solution.py:634
  71.8 20.2 %collective-permute-start.23 = (bf16[2,128,1024]{2,1,0:T(8,128)(2,1)S(1)}, bf16[2,128,1024]{2,1,0:T(8,128)(2,1)S(1)}, u32[]{:S(2)}, u32[]{:S(2)}) collective-permute-start(bf16[2,128,1024]{2,1,0:T(8,128)(2,1)S(1)} %collective-permute-done.7.refs_5_), channel_id=1, source_target_pairs={{0,4},{4,0},{8,12},{12,8},{16,20},{20,16},{24,28},{28,24},{1,5},{5... | collective-permute-start | bytes 1572872 | tf_op jit(solution)/shard_map/ppermute | solution.py:634
  71.9 20.9 %collective-permute-start.24 = (bf16[2,128,1024]{2,1,0:T(8,128)(2,1)}, bf16[2,128,1024]{2,1,0:T(8,128)(2,1)S(1)}, u32[]{:S(2)}, u32[]{:S(2)}) collective-permute-start(bf16[2,128,1024]{2,1,0:T(8,128)(2,1)} %collective-permute-done.8.refs_8_), channel_id=1, source_target_pairs={{0,4},{4,0},{8,12},{12,8},{16,20},{20,16},{24,28},{28,24},{1,5},{5... | collective-permute-start | bytes 1572872 | tf_op jit(solution)/shard_map/ppermute | solution.py:634
  72.4 21.8 %collective-permute-start.25 = (bf16[2,128,1024]{2,1,0:T(8,128)(2,1)}, bf16[2,128,1024]{2,1,0:T(8,128)(2,1)S(1)}, u32[]{:S(2)}, u32[]{:S(2)}) collective-permute-start(bf16[2,128,1024]{2,1,0:T(8,128)(2,1)} %copy-done.9), channel_id=1, source_target_pairs={{0,4},{4,0},{8,12},{12,8},{16,20},{20,16},{24,28},{28,24},{1,5},{5... | collective-permute-start | bytes 1572872 | tf_op jit(solution)/shard_map/ppermute | solution.py:634
  72.4 21.7 %collective-permute-start.10 = (bf16[2,128,1024]{2,1,0:T(8,128)(2,1)S(1)}, bf16[2,128,1024]{2,1,0:T(8,128)(2,1)}, u32[]{:S(2)}, u32[]{:S(2)}) collective-permute-start(bf16[2,128,1024]{2,1,0:T(8,128)(2,1)S(1)} %pad_maximum_fusion.1.refs_4_.refs_16_), channel_id=1, source_target_pairs={{0,16},{4,20},{8,24},{12,28},{16,0},{20,4},{24,8},{28,12},{1,17},{... | collective-permute-start | bytes 1572872 | tf_op jit(solution)/shard_map/ppermute | solution.py:634
  73.1 21.5 %collective-permute-start.12 = (bf16[2,128,1024]{2,1,0:T(8,128)(2,1)S(1)}, bf16[2,128,1024]{2,1,0:T(8,128)(2,1)S(1)}, u32[]{:S(2)}, u32[]{:S(2)}) collective-permute-start(bf16[2,128,1024]{2,1,0:T(8,128)(2,1)S(1)} %pad_maximum_fusion.2.refs_5_.refs_17_), channel_id=1, source_target_pairs={{0,8},{4,12},{8,0},{12,4},{16,24},{20,28},{24,16},{28,20},{1,9},{5... | collective-permute-start | bytes 1572872 | tf_op jit(solution)/shard_map/ppermute | solution.py:634
  92.0 14.9 %collective-permute-start.29 = (bf16[2,128,1024]{2,1,0:T(8,128)(2,1)S(1)}, bf16[2,128,1024]{2,1,0:T(8,128)(2,1)}, u32[]{:S(2)}, u32[]{:S(2)}) collective-permute-start(bf16[2,128,1024]{2,1,0:T(8,128)(2,1)S(1)} %pad_maximum_fusion.1.refs_4_.refs_16_), channel_id=1, source_target_pairs={{0,8},{4,12},{8,0},{12,4},{16,24},{20,28},{24,16},{28,20},{1,9},{5... | collective-permute-start | bytes 1572872 | tf_op jit(solution)/shard_map/ppermute | solution.py:634
  92.8 14.9 %collective-permute-start.32 = (bf16[2,128,1024]{2,1,0:T(8,128)(2,1)S(1)}, bf16[2,128,1024]{2,1,0:T(8,128)(2,1)}, u32[]{:S(2)}, u32[]{:S(2)}) collective-permute-start(bf16[2,128,1024]{2,1,0:T(8,128)(2,1)S(1)} %pad_maximum_fusion.2.refs_5_.refs_17_), channel_id=1, source_target_pairs={{0,16},{4,20},{8,24},{12,28},{16,0},{20,4},{24,8},{28,12},{1,17},{... | collective-permute-start | bytes 1572872 | tf_op jit(solution)/shard_map/ppermute | solution.py:634
  94.1 13.5 %collective-permute-start.26 = (bf16[2,128,1024]{2,1,0:T(8,128)(2,1)}, bf16[2,128,1024]{2,1,0:T(8,128)(2,1)}, u32[]{:S(2)}, u32[]{:S(2)}) collective-permute-start(bf16[2,128,1024]{2,1,0:T(8,128)(2,1)} %collective-permute-done.18.refs_12_), channel_id=1, source_target_pairs={{0,4},{4,0},{8,12},{12,8},{16,20},{20,16},{24,28},{28,24},{1,5},{5... | collective-permute-start | bytes 1572872 | tf_op jit(solution)/shard_map/ppermute | solution.py:634
  94.1 14.0 %collective-permute-start.27 = (bf16[2,128,1024]{2,1,0:T(8,128)(2,1)}, bf16[2,128,1024]{2,1,0:T(8,128)(2,1)}, u32[]{:S(2)}, u32[]{:S(2)}) collective-permute-start(bf16[2,128,1024]{2,1,0:T(8,128)(2,1)} %collective-permute-done.19.refs_13_), channel_id=1, source_target_pairs={{0,4},{4,0},{8,12},{12,8},{16,20},{20,16},{24,28},{28,24},{1,5},{5... | collective-permute-start | bytes 1572872 | tf_op jit(solution)/shard_map/ppermute | solution.py:634
  94.6 22.9 %collective-permute-start.11 = (bf16[2,128,1024]{2,1,0:T(8,128)(2,1)}, bf16[2,128,1024]{2,1,0:T(8,128)(2,1)}, u32[]{:S(2)}, u32[]{:S(2)}) collective-permute-start(bf16[2,128,1024]{2,1,0:T(8,128)(2,1)} %collective-permute-done.10.refs_4_.refs_24_), channel_id=1, source_target_pairs={{0,8},{4,12},{8,0},{12,4},{16,24},{20,28},{24,16},{28,20},{1,9},{5... | collective-permute-start | bytes 1572872 | tf_op jit(solution)/shard_map/ppermute | solution.py:634
  106.9 37.2 %collective-permute-start.13 = (bf16[2,128,1024]{2,1,0:T(8,128)(2,1)}, bf16[2,128,1024]{2,1,0:T(8,128)(2,1)S(1)}, u32[]{:S(2)}, u32[]{:S(2)}) collective-permute-start(bf16[2,128,1024]{2,1,0:T(8,128)(2,1)} %copy-done.13), channel_id=1, source_target_pairs={{0,16},{4,20},{8,24},{12,28},{16,0},{20,4},{24,8},{28,12},{1,17},{... | collective-permute-start | bytes 1572872 | tf_op jit(solution)/shard_map/ppermute | solution.py:634
  107.6 37.3 %collective-permute-start.31 = (bf16[2,128,1024]{2,1,0:T(8,128)(2,1)}, bf16[2,128,1024]{2,1,0:T(8,128)(2,1)S(1)}, u32[]{:S(2)}, u32[]{:S(2)}) collective-permute-start(bf16[2,128,1024]{2,1,0:T(8,128)(2,1)} %copy-done.13), channel_id=1, source_target_pairs={{0,4},{4,0},{8,12},{12,8},{16,20},{20,16},{24,28},{28,24},{1,5},{5... | collective-permute-start | bytes 1572872 | tf_op jit(solution)/shard_map/ppermute | solution.py:634
  107.6 37.8 %collective-permute-start.33 = (bf16[2,128,1024]{2,1,0:T(8,128)(2,1)}, bf16[2,128,1024]{2,1,0:T(8,128)(2,1)S(1)}, u32[]{:S(2)}, u32[]{:S(2)}) collective-permute-start(bf16[2,128,1024]{2,1,0:T(8,128)(2,1)} %collective-permute-done.10.refs_4_.refs_24_), channel_id=1, source_target_pairs={{0,4},{4,0},{8,12},{12,8},{16,20},{20,16},{24,28},{28,24},{1,5},{5... | collective-permute-start | bytes 1572872 | tf_op jit(solution)/shard_map/ppermute | solution.py:634
  108.1 36.7 %collective-permute-start.30 = (bf16[2,128,1024]{2,1,0:T(8,128)(2,1)}, bf16[2,128,1024]{2,1,0:T(8,128)(2,1)S(1)}, u32[]{:S(2)}, u32[]{:S(2)}) collective-permute-start(bf16[2,128,1024]{2,1,0:T(8,128)(2,1)} %collective-permute-done.29.refs_0_.refs_20_), channel_id=1, source_target_pairs={{0,4},{4,0},{8,12},{12,8},{16,20},{20,16},{24,28},{28,24},{1,5},{5... | collective-permute-start | bytes 1572872 | tf_op jit(solution)/shard_map/ppermute | solution.py:634
  117.6 27.9 %collective-permute-start.34 = (bf16[2,128,1024]{2,1,0:T(8,128)(2,1)}, bf16[2,128,1024]{2,1,0:T(8,128)(2,1)S(1)}, u32[]{:S(2)}, u32[]{:S(2)}) collective-permute-start(bf16[2,128,1024]{2,1,0:T(8,128)(2,1)} %collective-permute-done.32.refs_5_.refs_25_), channel_id=1, source_target_pairs={{0,4},{4,0},{8,12},{12,8},{16,20},{20,16},{24,28},{28,24},{1,5},{5... | collective-permute-start | bytes 1572872 | tf_op jit(solution)/shard_map/ppermute | solution.py:634
  144.2 29.5 %collective-permute-start.16 = (bf16[2,128,1024]{2,1,0:T(8,128)(2,1)S(1)}, bf16[2,128,1024]{2,1,0:T(8,128)(2,1)S(1)}, u32[]{:S(2)}, u32[]{:S(2)}) collective-permute-start(bf16[2,128,1024]{2,1,0:T(8,128)(2,1)S(1)} %pad_maximum_fusion.1.refs_4_.refs_16_), channel_id=1, source_target_pairs={{0,4},{4,0},{8,12},{12,8},{16,20},{20,16},{24,28},{28,24},{1,5},{5... | collective-permute-start | bytes 1572872 | tf_op jit(solution)/shard_map/ppermute | solution.py:634
  144.8 29.1 %collective-permute-start.17 = (bf16[2,128,1024]{2,1,0:T(8,128)(2,1)S(1)}, bf16[2,128,1024]{2,1,0:T(8,128)(2,1)}, u32[]{:S(2)}, u32[]{:S(2)}) collective-permute-start(bf16[2,128,1024]{2,1,0:T(8,128)(2,1)S(1)} %pad_maximum_fusion.2.refs_5_.refs_17_), channel_id=1, source_target_pairs={{0,4},{4,0},{8,12},{12,8},{16,20},{20,16},{24,28},{28,24},{1,5},{5... | collective-permute-start | bytes 1572872 | tf_op jit(solution)/shard_map/ppermute | solution.py:634
  144.9 29.0 %collective-permute-start.14 = (bf16[2,128,1024]{2,1,0:T(8,128)(2,1)}, bf16[2,128,1024]{2,1,0:T(8,128)(2,1)}, u32[]{:S(2)}, u32[]{:S(2)}) collective-permute-start(bf16[2,128,1024]{2,1,0:T(8,128)(2,1)} %collective-permute-done.11.refs_0_.refs_28_), channel_id=1, source_target_pairs={{0,4},{4,0},{8,12},{12,8},{16,20},{20,16},{24,28},{28,24},{1,5},{5... | collective-permute-start | bytes 1572872 | tf_op jit(solution)/shard_map/ppermute | solution.py:634
  145.4 28.6 %collective-permute-start.15 = (bf16[2,128,1024]{2,1,0:T(8,128)(2,1)S(1)}, bf16[2,128,1024]{2,1,0:T(8,128)(2,1)}, u32[]{:S(2)}, u32[]{:S(2)}) collective-permute-start(bf16[2,128,1024]{2,1,0:T(8,128)(2,1)S(1)} %collective-permute-done.13.refs_1_.refs_29_), channel_id=1, source_target_pairs={{0,4},{4,0},{8,12},{12,8},{16,20},{20,16},{24,28},{28,24},{1,5},{5... | collective-permute-start | bytes 1572872 | tf_op jit(solution)/shard_map/ppermute | solution.py:634
  173.3 54.2 %collective-permute-start.37 = (bf16[4,128,1024]{2,1,0:T(8,128)(2,1)}, bf16[4,128,1024]{2,1,0:T(8,128)(2,1)S(1)}, u32[]{:S(2)}, u32[]{:S(2)}) collective-permute-start(bf16[4,128,1024]{2,1,0:T(8,128)(2,1)} %get-tuple-element.58), channel_id=1, source_target_pairs={{0,4},{4,0},{8,12},{12,8},{16,20},{20,16},{24,28},{28,24},{1,5},{5... | collective-permute-start | bytes 3145736 | tf_op jit(solution)/shard_map/ppermute | solution.py:634
  173.7 56.4 %collective-permute-start.35 = (bf16[4,128,1024]{2,1,0:T(8,128)(2,1)}, bf16[4,128,1024]{2,1,0:T(8,128)(2,1)S(1)}, u32[]{:S(2)}, u32[]{:S(2)}) collective-permute-start(bf16[4,128,1024]{2,1,0:T(8,128)(2,1)} %get-tuple-element.56), channel_id=1, source_target_pairs={{0,4},{4,0},{8,12},{12,8},{16,20},{20,16},{24,28},{28,24},{1,5},{5... | collective-permute-start | bytes 3145736 | tf_op jit(solution)/shard_map/ppermute | solution.py:634
  201.6 57.9 %collective-permute-start.28 = (bf16[4,128,1024]{2,1,0:T(8,128)(2,1)}, bf16[4,128,1024]{2,1,0:T(8,128)(2,1)S(1)}, u32[]{:S(2)}, u32[]{:S(2)}) collective-permute-start(bf16[4,128,1024]{2,1,0:T(8,128)(2,1)} %get-tuple-element.54), channel_id=1, source_target_pairs={{0,4},{4,0},{8,12},{12,8},{16,20},{20,16},{24,28},{28,24},{1,5},{5... | collective-permute-start | bytes 3145736 | tf_op jit(solution)/shard_map/ppermute | solution.py:634
  208.3 20.6 %collective-permute-start.39 = (bf16[2,128,1024]{2,1,0:T(8,128)(2,1)S(1)}, bf16[2,128,1024]{2,1,0:T(8,128)(2,1)S(1)}, u32[]{:S(2)}, u32[]{:S(2)}) collective-permute-start(bf16[2,128,1024]{2,1,0:T(8,128)(2,1)S(1)} %get-tuple-element.75), channel_id=1, source_target_pairs={{0,8},{4,12},{8,0},{12,4},{16,24},{20,28},{24,16},{28,20},{1,9},{5... | collective-permute-start | bytes 1572872 | tf_op jit(solution)/shard_map/ppermute | solution.py:634
  209.1 17.6 %collective-permute-start.48 = (f32[8,48,128]{2,1,0:T(8,128)S(1)}, f32[8,48,128]{2,1,0:T(8,128)S(1)}, u32[]{:S(2)}, u32[]{:S(2)}) collective-permute-start(f32[8,48,128]{2,1,0:T(8,128)S(1)} %bitcast.116), channel_id=1, source_target_pairs={{0,8},{4,12},{8,0},{12,4},{16,24},{20,28},{24,16},{28,20},{1,9},{5... | collective-permute-start | bytes 589832 | tf_op jit(solution)/shard_map/ppermute | solution.py:634
  226.8 14.9 %collective-permute-start.42 = (bf16[2,128,1024]{2,1,0:T(8,128)(2,1)S(1)}, bf16[2,128,1024]{2,1,0:T(8,128)(2,1)S(1)}, u32[]{:S(2)}, u32[]{:S(2)}) collective-permute-start(bf16[2,128,1024]{2,1,0:T(8,128)(2,1)S(1)} %get-tuple-element.76), channel_id=1, source_target_pairs={{0,16},{4,20},{8,24},{12,28},{16,0},{20,4},{24,8},{28,12},{1,17},{... | collective-permute-start | bytes 1572872 | tf_op jit(solution)/shard_map/ppermute | solution.py:634
  227.4 18.4 %collective-permute-start.49 = (f32[8,48,128]{2,1,0:T(8,128)S(1)}, f32[8,48,128]{2,1,0:T(8,128)S(1)}, u32[]{:S(2)}, u32[]{:S(2)}) collective-permute-start(f32[8,48,128]{2,1,0:T(8,128)S(1)} %bitcast.114), channel_id=1, source_target_pairs={{0,16},{4,20},{8,24},{12,28},{16,0},{20,4},{24,8},{28,12},{1,17},{... | collective-permute-start | bytes 589832 | tf_op jit(solution)/shard_map/ppermute | solution.py:634
  229.4 30.1 %collective-permute-start.40 = (bf16[2,128,1024]{2,1,0:T(8,128)(2,1)S(1)}, bf16[2,128,1024]{2,1,0:T(8,128)(2,1)S(1)}, u32[]{:S(2)}, u32[]{:S(2)}) collective-permute-start(bf16[2,128,1024]{2,1,0:T(8,128)(2,1)S(1)} %get-tuple-element.73), channel_id=1, source_target_pairs={{0,16},{4,20},{8,24},{12,28},{16,0},{20,4},{24,8},{28,12},{1,17},{... | collective-permute-start | bytes 1572872 | tf_op jit(solution)/shard_map/ppermute | solution.py:634
  242.1 17.4 %collective-permute-start.36 = (bf16[2,128,1024]{2,1,0:T(8,128)(2,1)S(1)}, bf16[2,128,1024]{2,1,0:T(8,128)(2,1)S(1)}, u32[]{:S(2)}, u32[]{:S(2)}) collective-permute-start(bf16[2,128,1024]{2,1,0:T(8,128)(2,1)S(1)} %get-tuple-element.71), channel_id=1, source_target_pairs={{0,8},{4,12},{8,0},{12,4},{16,24},{20,28},{24,16},{28,20},{1,9},{5... | collective-permute-start | bytes 1572872 | tf_op jit(solution)/shard_map/ppermute | solution.py:634
  242.9 23.9 %collective-permute-start.44 = (bf16[2,128,1024]{2,1,0:T(8,128)(2,1)S(1)}, bf16[2,128,1024]{2,1,0:T(8,128)(2,1)S(1)}, u32[]{:S(2)}, u32[]{:S(2)}) collective-permute-start(bf16[2,128,1024]{2,1,0:T(8,128)(2,1)S(1)} %get-tuple-element.74), channel_id=1, source_target_pairs={{0,16},{4,20},{8,24},{12,28},{16,0},{20,4},{24,8},{28,12},{1,17},{... | collective-permute-start | bytes 1572872 | tf_op jit(solution)/shard_map/ppermute | solution.py:634
  245.8 21.0 %collective-permute-start.43 = (bf16[2,128,1024]{2,1,0:T(8,128)(2,1)S(1)}, bf16[2,128,1024]{2,1,0:T(8,128)(2,1)}, u32[]{:S(2)}, u32[]{:S(2)}) collective-permute-start(bf16[2,128,1024]{2,1,0:T(8,128)(2,1)S(1)} %get-tuple-element.72), channel_id=1, source_target_pairs={{0,8},{4,12},{8,0},{12,4},{16,24},{20,28},{24,16},{28,20},{1,9},{5... | collective-permute-start | bytes 1572872 | tf_op jit(solution)/shard_map/ppermute | solution.py:634
  268.8 11.2 %collective-permute-start.46 = (bf16[128,1024]{1,0:T(8,128)(2,1)S(1)}, bf16[128,1024]{1,0:T(8,128)(2,1)S(1)}, u32[]{:S(2)}, u32[]{:S(2)}) collective-permute-start(bf16[128,1024]{1,0:T(8,128)(2,1)S(1)} %get-tuple-element.80), channel_id=1, source_target_pairs={{0,3},{1,2},{2,1},{3,0},{4,7},{5,6},{6,5},{7,4},{8,11},{9,10},{10,... | collective-permute-start | bytes 786440 | tf_op jit(solution)/shard_map/ppermute | solution.py:634
  271.1 20.4 %collective-permute-start.45 = (bf16[128,1024]{1,0:T(8,128)(2,1)S(1)}, bf16[128,1024]{1,0:T(8,128)(2,1)S(1)}, u32[]{:S(2)}, u32[]{:S(2)}) collective-permute-start(bf16[128,1024]{1,0:T(8,128)(2,1)S(1)} %get-tuple-element.79), channel_id=1, source_target_pairs={{0,2},{1,3},{2,0},{3,1},{4,6},{5,7},{6,4},{7,5},{8,10},{9,11},{10,... | collective-permute-start | bytes 786440 | tf_op jit(solution)/shard_map/ppermute | solution.py:634
  271.1 20.4 %collective-permute-start.41 = (bf16[128,1024]{1,0:T(8,128)(2,1)S(1)}, bf16[128,1024]{1,0:T(8,128)(2,1)S(1)}, u32[]{:S(2)}, u32[]{:S(2)}) collective-permute-start(bf16[128,1024]{1,0:T(8,128)(2,1)S(1)} %slice_bitcast_fusion.2), channel_id=1, source_target_pairs={{0,1},{1,0},{2,3},{3,2},{4,5},{5,4},{6,7},{7,6},{8,9},{9,8},{10,11... | collective-permute-start | bytes 786440 | tf_op jit(solution)/shard_map/ppermute | solution.py:634
  (28 other events, 918.0 us)
